TPU v7x, 128 devices: a whole 4x4x4 slice. The times are simulated.
128 devices in a mesh: gx: 64 (over z, x, y), gy: 2 (over core).
Axes of the slice: x: 4, y: 4, z: 4, core: 2. Of those that a mesh axis runs over, the one named last changes fastest.
Arguments:
- field: bfloat16 [1, 64, 2048, 2048], P(None, None, 'gx', 'gy'), may hold values from -6 to 6
- cotangent: bfloat16 [1, 64, 2048, 2048], P(None, None, 'gx', 'gy'), may hold values from -6 to 6
- local_weight: bfloat16 [64, 64], replicated, may hold values from -0.75 to 0.75
- spectral_weight: bfloat16 [64, 64, 64, 128], P('gx', 'gy'), may hold values from -0.5 to 0.5
Outputs:
- grad_field: bfloat16 [1, 64, 2048, 2048], P(None, None, 'gx', 'gy')
- grad_spectral: float32 [64, 64, 64, 128], P('gx', 'gy')
- grad_local: float32 [64, 64], replicated
All inputs are finite; a program needn't handle non-finite values.
Results may differ from a plain program's by a relative error of at most 0.023.
Values may be sent and summed in bfloat16 or wider, within the bound.
No kernel may reach another device: no remote copies, remote signals or barrier semaphores. Data moves between devices by JAX's collectives and lax.ppermute only.
A program may use at most 128 MiB of HBM per device.

v0:
```python
import math

import jax
import jax.experimental.pallas as pl
import jax.experimental.pallas.tpu as pltpu
import jax.numpy as jnp
import numpy as np
from jax import lax
from jax.sharding import PartitionSpec as P

NX = 2048
NY = 2048
C = 64
MX = 64
MY = 64
SHARDS = 64
XC = 32
YC = 1024
YB = 256
TWO_PI = 2.0 * math.pi
ROOT_HALF = 1.0 / math.sqrt(2.0)
ROOT_TWO_PI = 1.0 / math.sqrt(2.0 * math.pi)
FORWARD = 1.0 / math.sqrt(NX * NY)
INVERSE = 1.0 / math.sqrt(MX * MY)
GAMMA = math.sqrt(MX * MY / (NX * NY))
BF = jnp.bfloat16
F32 = jnp.float32
RIDER = 8


def tables():
    angle = (np.arange(YC)[:, None] * np.arange(MY)[None, :] % NY) * (TWO_PI / NY)
    pair = np.stack([np.cos(angle), -np.sin(angle)], axis=1).reshape(YC, 2, 2, 32)
    forth = np.transpose(pair, (0, 2, 1, 3)).reshape(YC, 128)
    back = forth.T.reshape(2, 1, 64, YC)
    back = np.concatenate([back, back], axis=1).reshape(256, YC)
    modes = np.arange(MX)
    frequency = np.where(modes < MX // 2, modes, modes + NX - MX)
    xangle = (frequency[:, None] * np.arange(NX)[None, :] % NX) * (TWO_PI / NX)
    phase = np.stack([np.cos(xangle), np.sin(xangle)]).reshape(2, MX, SHARDS, XC)
    return forth, back, np.transpose(phase, (2, 0, 1, 3)), np.transpose(phase, (2, 0, 3, 1))


def dot(a, b, dims=((1,), (0,))):
    return lax.dot_general(a, b, (dims, ((), ())), preferred_element_type=F32)


def iota(shape, axis):
    return lax.broadcasted_iota(jnp.int32, shape, axis)


def turn(values, sign):
    lane = iota(values.shape, 1)
    first = lane % 64 < 32
    return jnp.where(first, sign * pltpu.roll(values, 96, 1), -sign * pltpu.roll(values, 32, 1))


def parity(core, shape):
    return jnp.where((iota(shape, len(shape) - 1) % 2) * core == 1, -1.0, 1.0).astype(F32)


def split_halves(parts, cells, groups, core, own_ref, other_ref):
    rows = cells * groups * 8
    blocks = parts.reshape(cells * groups, 2, 8, 128)
    first = blocks[:, 0].reshape(rows, 128)
    second = blocks[:, 1].reshape(rows, 128)
    low = iota((rows, 128), 1) < 64
    sign = parity(core, (rows, 128))
    half_a = jnp.where(low, first, pltpu.roll(second, 64, 1)) * sign
    half_b = jnp.where(low, pltpu.roll(first, 64, 1), second) * sign
    own = jnp.where(core == 0, half_a, half_b)
    other = jnp.where(core == 0, half_b, half_a)
    own_ref[...] = own.reshape(cells, groups * 8, 128).astype(BF)
    other_ref[...] = other.reshape(cells, groups * 8, 128).astype(BF)


def y_forward_kernel(place, field_ref, forth_ref, cells_ref, own_ref, other_ref):
    rows = jnp.swapaxes(field_ref[...], 0, 1)
    cells_ref[...] = rows
    parts = dot(rows.reshape(16 * 32, YC), forth_ref[...])
    split_halves(parts, 16, 2, place[1], own_ref, other_ref)


def y_forward(place, field, forth):
    part = pl.BlockSpec((16, 16, 128), lambda g, h, s: (h, g, 0))
    return pl.pallas_call(
        y_forward_kernel,
        grid_spec=pltpu.PrefetchScalarGridSpec(
            num_scalar_prefetch=1,
            grid=(2, 2),
            in_specs=[
                pl.BlockSpec((32, 16, YC), lambda g, h, s: (g, h, 0)),
                pl.BlockSpec((YC, 128), lambda g, h, s: (0, 0)),
            ],
            out_specs=[pl.BlockSpec((16, 32, YC), lambda g, h, s: (h, g, 0)), part, part],
        ),
        out_shape=[
            jax.ShapeDtypeStruct((XC, C, YC), BF),
            jax.ShapeDtypeStruct((XC, 32, 128), BF),
            jax.ShapeDtypeStruct((XC, 32, 128), BF),
        ],
        compiler_params=pltpu.CompilerParams(vmem_limit_bytes=20 << 20),
        name="y_forward",
    )(place, field, forth)


def x_forward_kernel(scale, place, phase_ref, own_ref, other_ref, *rest):
    out_ref = rest[-1]
    total = own_ref[...].astype(F32) + other_ref[...].astype(F32)
    widen = (iota((XC, 256), 1) // 8 == iota((XC, 256), 0)).astype(BF)
    keep = iota((1, 8, 256), 2) % 8 == iota((1, 8, 256), 1)
    left = []
    for q in range(2):
        wide = dot(phase_ref[0, q], widen)
        left.append(jnp.where(keep, wide[:, None, :], 0.0).reshape(512, 256).astype(BF))
    left = jnp.concatenate(left, axis=1)
    for g in range(2):
        right = []
        for s in range(2):
            rows = total[:, 16 * g + 8 * s : 16 * g + 8 * s + 8].reshape(256, 128)
            right.append(jnp.concatenate([rows, turn(rows, 1.0)], axis=0))
        modes = dot(left, jnp.concatenate(right, axis=1).astype(BF)) * scale
        both = [modes[:, 128 * s : 128 * s + 128].reshape(64, 8, 128) for s in range(2)]
        out_ref[:, 16 * g : 16 * g + 16, :] = jnp.concatenate(both, axis=1).astype(BF)
    if len(rest) == 2:
        rider = rest[0][...].astype(F32)
        out_ref[:, 32:, :] = jnp.broadcast_to(rider[:, None, :], (64, RIDER, 128)).astype(BF)


def x_forward(place, phase, own, other, scale, rider=None):
    rows = 32 if rider is None else 32 + RIDER
    operands = [own, other] + ([] if rider is None else [rider])

    def whole(a):
        return pl.BlockSpec(a.shape, lambda i, s: (0,) * a.ndim)

    return pl.pallas_call(
        lambda *refs: x_forward_kernel(scale, *refs),
        grid_spec=pltpu.PrefetchScalarGridSpec(
            num_scalar_prefetch=1,
            grid=(1,),
            in_specs=[pl.BlockSpec((1, 2, MX, XC), lambda i, s: (s[0], 0, 0, 0))]
            + [whole(a) for a in operands],
            out_specs=pl.BlockSpec((SHARDS, rows, 128), lambda i, s: (0, 0, 0)),
        ),
        out_shape=jax.ShapeDtypeStruct((SHARDS, rows, 128), BF),
        compiler_params=pltpu.CompilerParams(vmem_limit_bytes=20 << 20),
        name="x_forward",
    )(place, phase, *operands)


def x_inverse_kernel(place, phase_ref, sent_ref, inner_ref):
    widen = (iota((MX, 512), 1) // 8 == iota((MX, 512), 0)).astype(BF)
    keep = iota((1, 8, 512), 2) % 8 == iota((1, 8, 512), 1)
    left = []
    for q in range(2):
        wide = dot(phase_ref[0, q], widen)
        left.append(jnp.where(keep, wide[:, None, :], 0.0).reshape(256, 512).astype(BF))
    left = jnp.concatenate(left, axis=0)
    for g in range(2):
        rows = sent_ref[:, 16 * g : 16 * g + 16, :].astype(F32)
        right = [rows[:, 8 * s : 8 * s + 8].reshape(512, 128) for s in range(2)]
        both = dot(left, jnp.concatenate(right, axis=1).astype(BF))
        inner = []
        for s in range(2):
            piece = both[:, 128 * s : 128 * s + 128]
            inner.append((piece[:256] + turn(piece[256:], -1.0)).reshape(XC, 8, 128))
        inner_ref[:XC, 16 * g : 16 * g + 16, :] = jnp.concatenate(inner, axis=1).astype(BF)
    if sent_ref.shape[1] > 32:
        rider = sent_ref[:, 32:, :].astype(F32)[:, 0, :]
        inner_ref[XC:, :, :] = rider.reshape(2, 32, 128).astype(BF)


def x_inverse(place, phase, sent):
    cells = XC if sent.shape[1] == 32 else XC + 2
    return pl.pallas_call(
        x_inverse_kernel,
        grid_spec=pltpu.PrefetchScalarGridSpec(
            num_scalar_prefetch=1,
            grid=(1,),
            in_specs=[
                pl.BlockSpec((1, 2, XC, MX), lambda i, s: (s[0], 0, 0, 0)),
                pl.BlockSpec(sent.shape, lambda i, s: (0, 0, 0)),
            ],
            out_specs=pl.BlockSpec((cells, 32, 128), lambda i, s: (0, 0, 0)),
        ),
        out_shape=jax.ShapeDtypeStruct((cells, 32, 128), BF),
        compiler_params=pltpu.CompilerParams(vmem_limit_bytes=20 << 20),
        name="x_inverse",
    )(place, phase, sent)


def pick(b):
    r = iota((32, C), 0)
    return (iota((32, C), 1) == (r // 8) * 16 + b * 8 + r % 8).astype(BF)


def modes_of(rows):
    flipped = rows.T.astype(BF)
    return (dot(flipped[:64], pick(0)) + dot(flipped[64:], pick(1))).astype(BF)


def rows_of(real, imag):
    blocks = [dot(pick(b), part, ((1,), (1,))) for b in range(2) for part in (real, imag)]
    return jnp.concatenate(blocks, axis=1)


def own_mode(shape):
    return iota(shape, 1) // C == iota(shape, 0) % 32


def mix_kernel(sent_ref, weight_ref, out_ref, spectrum_ref):
    spectrum = modes_of(jnp.sum(sent_ref[...].astype(F32), axis=0))
    spectrum_ref[...] = spectrum
    pair = spectrum.astype(F32)
    pair = jnp.concatenate([pair, pair], axis=1)
    wide = jnp.concatenate([pair] * 16, axis=1)
    wide = jnp.where(own_mode(wide.shape), wide, 0.0).astype(BF)
    product = dot(wide, weight_ref[...].reshape(32 * C, 128))
    lane = iota((32, 128), 1)
    mixed = product[:32] + jnp.where(lane < 64, -1.0, 1.0) * pltpu.roll(product[32:], 64, 1)
    mixed = mixed.astype(BF)
    rows = rows_of(mixed[:, :64], mixed[:, 64:])
    out_ref[...] = jnp.broadcast_to(rows[None], (SHARDS, 32, 128)).astype(BF)


def mix(sent, weights):
    return pl.pallas_call(
        mix_kernel,
        out_shape=[
            jax.ShapeDtypeStruct((SHARDS, 32, 128), BF),
            jax.ShapeDtypeStruct((64, C), BF),
        ],
        compiler_params=pltpu.CompilerParams(vmem_limit_bytes=20 << 20),
        name="mix",
    )(sent, weights)


def mix_back_kernel(sent_ref, weight_ref, out_ref, pair_ref):
    total = jnp.sum(sent_ref[...].astype(F32), axis=0)
    modes = modes_of(total[:32]).astype(F32)
    real, imag = modes[:32], modes[32:]
    left = jnp.concatenate([real, imag], axis=1)
    right = jnp.concatenate([imag, -real], axis=1)
    pair = jnp.concatenate([left, right], axis=0).astype(BF)
    pair_ref[...] = pair
    product = dot(pair, weight_ref[...].reshape(32 * C, 128), ((1,), (1,)))
    product = jnp.where(own_mode(product.shape), product, 0.0)
    folded = product[:, :128]
    for k in range(1, 16):
        folded = folded + product[:, 128 * k : 128 * k + 128]
    folded = (folded + pltpu.roll(folded, 64, 1))[:, :64].astype(BF)
    rows = rows_of(folded[:32], folded[32:])
    rider = total[32:]
    rider = rider + pltpu.roll(rider, 64, 1)
    high = rider.astype(BF).astype(F32)
    rider = jnp.where(iota(rider.shape, 1) < 64, high, rider - high)
    rows = jnp.concatenate([rows, rider], axis=0)
    out_ref[...] = jnp.broadcast_to(rows[None], (SHARDS, 32 + RIDER, 128)).astype(BF)


def mix_back(sent, weights):
    return pl.pallas_call(
        mix_back_kernel,
        out_shape=[
            jax.ShapeDtypeStruct((SHARDS, 32 + RIDER, 128), BF),
            jax.ShapeDtypeStruct((64, 128), BF),
        ],
        compiler_params=pltpu.CompilerParams(vmem_limit_bytes=20 << 20),
        name="mix_back",
    )(sent, weights)


def outer_kernel(spectrum_ref, pair_ref, out_ref):
    flipped = spectrum_ref[...].astype(F32).T
    tall = jnp.concatenate([flipped] * 8, axis=0)
    shape = tall.shape
    keep = iota(shape, 1) % 32 == iota(shape, 0) // C + 8 * pl.program_id(0)
    tall = jnp.where(keep, tall, 0.0).astype(BF)
    out_ref[...] = (dot(tall, pair_ref[...]) * GAMMA).reshape(8, C, 128)


def outer(spectrum, pair):
    return pl.pallas_call(
        outer_kernel,
        grid=(4,),
        in_specs=[pl.BlockSpec((64, C), lambda i: (0, 0)), pl.BlockSpec((64, 128), lambda i: (0, 0))],
        out_specs=pl.BlockSpec((8, C, 128), lambda i: (i, 0, 0)),
        out_shape=jax.ShapeDtypeStruct((32, C, 128), F32),
        compiler_params=pltpu.CompilerParams(vmem_limit_bytes=20 << 20),
        cost_estimate=pl.CostEstimate(flops=2 * 2048 * 64 * 128, bytes_accessed=1 << 20, transcendentals=0),
        name="outer",
    )(spectrum, pair)


def gelu_slope(values):
    return (
        0.5 * (1.0 + lax.erf(values * ROOT_HALF))
        + values * jnp.exp(-0.5 * values * values) * ROOT_TWO_PI
    )


def block_diagonal(square):
    wide = jnp.concatenate([square, square], axis=1)
    wide = jnp.concatenate([wide, wide], axis=1)
    full = jnp.concatenate([wide] * 4, axis=0)
    return jnp.where(iota(full.shape, 0) // C == iota(full.shape, 1) // C, full, 0.0)


def inner_rows(core, scale, own_ref, other_ref, rows_ref):
    own = own_ref[...].astype(F32)
    other = other_ref[...].astype(F32)
    shape = own.shape
    sign = parity(core, shape) * scale
    for half in range(2):
        values = jnp.where(core == half, own, other) * sign
        values = values.reshape(shape[0] * 4, 8, 128)
        low = iota(values.shape, 2) < 64
        first = jnp.where(low, values, 0.0)
        second = values - first
        both = jnp.stack([first, second], axis=1).reshape(shape[0] * C, 128)
        rows_ref[:, 128 * half : 128 * half + 128] = both.astype(BF)


def cells_kernel(
    place,
    field_ref,
    cotangent_ref,
    own_in_ref,
    other_in_ref,
    local_ref,
    forth_ref,
    back_ref,
    slope_ref,
    own_ref,
    other_ref,
    weight_ref,
    diagonal,
    inner,
    parts,
    products,
):
    half, block = pl.program_id(0), pl.program_id(1)

    @pl.when(jnp.logical_and(half == 0, block == 0))
    def _():
        diagonal[...] = block_diagonal(local_ref[...].astype(F32)).T.astype(BF)
        products[...] = jnp.zeros_like(products)

    @pl.when(block == 0)
    def _():
        inner_rows(place[1], INVERSE, own_in_ref, other_in_ref, inner)
        parts[...] = jnp.zeros_like(parts)

    cotangent = jnp.swapaxes(cotangent_ref[...], 0, 1)
    for g in range(4):
        rows = slice(256 * g, 256 * g + 256)
        field = field_ref[4 * g : 4 * g + 4].reshape(256, YB)
        pre_act = dot(diagonal[...], field) + dot(inner[rows, :], back_ref[...])
        upper = cotangent[4 * g : 4 * g + 4].reshape(256, YB).astype(F32)
        slope = (upper * gelu_slope(pre_act)).astype(BF)
        slope_ref[4 * g : 4 * g + 4] = slope.reshape(4, C, YB)
        products[...] += dot(field, slope, ((1,), (1,)))
        parts[rows, :] += dot(slope, forth_ref[...])

    @pl.when(block == YC // YB - 1)
    def _():
        split_halves(parts[...], 16, 4, place[1], own_ref, other_ref)

    @pl.when(jnp.logical_and(half == 1, block == YC // YB - 1))
    def _():
        total = products[...]
        first = total[:64, :128] + pltpu.roll(total[64:128, :128], 64, 1)
        first = first + total[128:192, 128:] + pltpu.roll(total[192:, 128:], 64, 1)
        high = first.astype(BF).astype(F32)
        low = pltpu.roll(first - high, 64, 1)
        weight_ref[...] = jnp.where(iota((64, 128), 1) < 64, high, low).astype(BF)


def cells_step(place, cells, cotangent, own, other, local_weight, forth, back):
    part = pl.BlockSpec((16, 32, 128), lambda h, i, s: (h, 0, 0))
    return pl.pallas_call(
        cells_kernel,
        grid_spec=pltpu.PrefetchScalarGridSpec(
            num_scalar_prefetch=1,
            grid=(2, YC // YB),
            in_specs=[
                pl.BlockSpec((16, C, YB), lambda h, i, s: (h, 0, i)),
                pl.BlockSpec((C, 16, YB), lambda h, i, s: (0, h, i)),
                part,
                part,
                pl.BlockSpec((C, C), lambda h, i, s: (0, 0)),
                pl.BlockSpec((YB, 128), lambda h, i, s: (i, 0)),
                pl.BlockSpec((256, YB), lambda h, i, s: (0, i)),
            ],
            out_specs=[
                pl.BlockSpec((16, C, YB), lambda h, i, s: (h, 0, i)),
                part,
                part,
                pl.BlockSpec((64, 128), lambda h, i, s: (0, 0)),
            ],
            scratch_shapes=[
                pltpu.VMEM((256, 256), BF),
                pltpu.VMEM((1024, 256), BF),
                pltpu.VMEM((1024, 128), F32),
                pltpu.VMEM((256, 256), F32),
            ],
        ),
        out_shape=[
            jax.ShapeDtypeStruct((XC, C, YC), BF),
            jax.ShapeDtypeStruct((XC, 32, 128), BF),
            jax.ShapeDtypeStruct((XC, 32, 128), BF),
            jax.ShapeDtypeStruct((64, 128), BF),
        ],
        compiler_params=pltpu.CompilerParams(vmem_limit_bytes=24 << 20),
        name="cells_step",
    )(place, cells, cotangent, own, other, local_weight, forth, back)


def last_kernel(
    place,
    slope_ref,
    own_in_ref,
    other_in_ref,
    own_tail_ref,
    other_tail_ref,
    local_ref,
    back_ref,
    out_ref,
    grad_local_ref,
    diagonal,
    inner,
):
    half, block = pl.program_id(0), pl.program_id(1)

    @pl.when(jnp.logical_and(half == 0, block == 0))
    def _():
        diagonal[...] = block_diagonal(local_ref[...].astype(F32)).astype(BF)
        total = own_tail_ref[...].astype(F32).reshape(64, 128)
        total = total + pltpu.roll(total, 64, 1)
        more = other_tail_ref[...].astype(F32).reshape(64, 128)
        more = more + pltpu.roll(more, 64, 1)
        grad_local_ref[...] = (total + more)[:, :64] * FORWARD

    @pl.when(block == 0)
    def _():
        inner_rows(place[1], FORWARD, own_in_ref, other_in_ref, inner)

    pieces = []
    for g in range(4):
        rows = slice(256 * g, 256 * g + 256)
        slope = slope_ref[4 * g : 4 * g + 4].reshape(256, YB)
        total = dot(diagonal[...], slope) + dot(inner[rows, :], back_ref[...])
        pieces.append(total.astype(BF).reshape(4, C, YB))
    out_ref[...] = jnp.swapaxes(jnp.concatenate(pieces, axis=0), 0, 1)


def last_step(place, slope, own, other, local_weight, back):
    part = pl.BlockSpec((16, 32, 128), lambda h, i, s: (h, 0, 0))
    tail = pl.BlockSpec((2, 32, 128), lambda h, i, s: (XC // 2, 0, 0))
    return pl.pallas_call(
        last_kernel,
        grid_spec=pltpu.PrefetchScalarGridSpec(
            num_scalar_prefetch=1,
            grid=(2, YC // YB),
            in_specs=[
                pl.BlockSpec((16, C, YB), lambda h, i, s: (h, 0, i)),
                part,
                part,
                tail,
                tail,
                pl.BlockSpec((C, C), lambda h, i, s: (0, 0)),
                pl.BlockSpec((256, YB), lambda h, i, s: (0, i)),
            ],
            out_specs=[
                pl.BlockSpec((C, 16, YB), lambda h, i, s: (0, h, i)),
                pl.BlockSpec((C, C), lambda h, i, s: (0, 0)),
            ],
            scratch_shapes=[pltpu.VMEM((256, 256), BF), pltpu.VMEM((1024, 256), BF)],
        ),
        out_shape=[
            jax.ShapeDtypeStruct((C, XC, YC), BF),
            jax.ShapeDtypeStruct((C, C), F32),
        ],
        compiler_params=pltpu.CompilerParams(vmem_limit_bytes=24 << 20),
        name="last_step",
    )(place, slope, own, other, own, other, local_weight, back)


def swap_cores(values):
    return lax.ppermute(values, "gy", [(0, 1), (1, 0)])


def exchange(rows):
    return lax.all_to_all(rows, "gx", 0, 0, tiled=True)


def on_device(field, cotangent, local_weight, spectral_weight):
    forth, back, phase, phase_back = [jnp.asarray(t.astype(np.float32), BF) for t in tables()]
    place = jnp.stack([lax.axis_index("gx"), lax.axis_index("gy")]).astype(jnp.int32)
    weights = spectral_weight[0]

    cells, own, other = y_forward(place, field[0], forth)
    sent = exchange(x_forward(place, phase, own, swap_cores(other), FORWARD))
    copies, spectrum = mix(sent, weights)
    inner = x_inverse(place, phase_back, exchange(copies))
    slope, own, other, rider = cells_step(
        place, cells, cotangent[0], inner, swap_cores(inner), local_weight, forth, back
    )
    sent = exchange(x_forward(place, phase, own, swap_cores(other), INVERSE, rider))
    copies, pair = mix_back(sent, weights)
    inner = x_inverse(place, phase_back, exchange(copies))
    grad_spectral = outer(spectrum, pair)
    grad_field, grad_local = last_step(place, slope, inner, swap_cores(inner), local_weight, back)
    return (grad_field[None], grad_spectral[None], grad_local)


def solution(mesh):
    placed = (P(None, None, "gx", "gy"), P(None, None, "gx", "gy"), P(), P("gx", "gy", None, None))
    return jax.shard_map(
        on_device,
        mesh=mesh,
        in_specs=placed,
        out_specs=(P(None, None, "gx", "gy"), P("gx", "gy", None, None), P()),
        check_vma=False,
    )
```

profile of v0, /device:TPU:1, one launch (start us, length us, event | category | flops | bytes accessed | tf_op | source)
XLA Modules:
  0.0 121.8 jit_solution(10256204468488915563)
XLA Ops:
  0.6 0.1 pad_add_fusion.place.refs_0_
  0.7 2.3 %copy-done.2 = bf16[1,64,32,1024]{3,2,1,0:T(8,128)(2,1)S(1)} copy-done((bf16[1,64,32,1024]{3,2,1,0:T(8,128)(2,1)S(1)}, bf16[1,64,32,1024]{3,2,1,0:T(8,128)(2,1)}, u32[]{:S(2)}) %copy-start.2) | copy-done | bytes 4194328
  3.0 0.9 copy-done.6
  4.0 3.3 %y_forward.1 = (bf16[32,64,1024]{2,1,0:T(8,128)(2,1)S(1)}, bf16[32,32,128]{2,1,0:T(8,128)(2,1)S(1)}, bf16[32,32,128]{2,1,0:T(8,128)(2,1)S(1)}) custom-call(s32[2]{0:T(128)S(1)} %pad_add_fusion.place.refs_0_, bf16[64,32,1024]{2,1,0:T(8,128)(2,1)S(1)} %bitcast.8, bf16[1024,128]{1,0:T(8,128)(2,1)S(1)} %copy-done.6), custom_call_target="tpu_custom_call" | custom-call | tf_op jit(solution)/shard_map/y_forward/pallas_call | solution.py:86
  7.4 1.5 %collective-permute-start = (bf16[32,32,128]{2,1,0:T(8,128)(2,1)S(1)}, bf16[32,32,128]{2,1,0:T(8,128)(2,1)S(1)}, u32[]{:S(2)}, u32[]{:S(2)}) collective-permute-start(bf16[32,32,128]{2,1,0:T(8,128)(2,1)S(1)} %get-tuple-element.18), channel_id=1, source_target_pairs={{0,1},{1,0},{2,3},{3,2},{4,5},{5,4},{6,7},{7,6},{8,9},{9,8},{10,11... | collective-permute-start | bytes 786440 | tf_op jit(solution)/shard_map/ppermute | solution.py:491
  8.9 1.2 collective-permute-done.refs_3_
  10.0 1.1 x_forward.2
  11.1 23.2 %all_to_all.20.sent_ref = bf16[64,32,128]{2,1,0:T(8,128)(2,1)S(1)} all-to-all(bf16[64,32,128]{2,1,0:T(8,128)(2,1)S(1)} %x_forward.2), channel_id=1, replica_groups=mesh['gx'=64,'gy'=2] {'gx'}, dimensions={0} | all-to-all | bytes 1048576 | tf_op jit(solution)/shard_map/all_to_all | solution.py:495
  34.4 1.0 mix.1
  35.4 15.4 %all_to_all.21.sent_ref = bf16[64,32,128]{2,1,0:T(8,128)(2,1)S(1)} all-to-all(bf16[64,32,128]{2,1,0:T(8,128)(2,1)S(1)} %get-tuple-element.19), channel_id=1, replica_groups=mesh['gx'=64,'gy'=2] {'gx'}, dimensions={0} | all-to-all | bytes 1048576 | tf_op jit(solution)/shard_map/all_to_all | solution.py:495
  50.8 1.4 %x_inverse.2.own_in_ref = bf16[32,32,128]{2,1,0:T(8,128)(2,1)S(1)} custom-call(s32[2]{0:T(128)S(1)} %pad_add_fusion.place.refs_0_, bf16[64,2,32,64]{3,2,1,0:T(8,128)(2,1)S(1)} %copy-done.3, bf16[64,32,128]{2,1,0:T(8,128)(2,1)S(1)} %all_to_all.21.sent_ref), custom_call_target="tpu_custom_call" | custom-call | tf_op jit(solution)/shard_map/x_inverse/pallas_call | solution.py:176
  52.2 3.4 %collective-permute-start.1 = (bf16[32,32,128]{2,1,0:T(8,128)(2,1)S(1)}, bf16[32,32,128]{2,1,0:T(8,128)(2,1)S(1)}, u32[]{:S(2)}, u32[]{:S(2)}) collective-permute-start(bf16[32,32,128]{2,1,0:T(8,128)(2,1)S(1)} %x_inverse.2.own_in_ref), channel_id=1, source_target_pairs={{0,1},{1,0},{2,3},{3,2},{4,5},{5,4},{6,7},{7,6},{8,9},{9,8},{10,11... | collective-permute-start | bytes 786440 | tf_op jit(solution)/shard_map/ppermute | solution.py:491
  55.5 1.2 collective-permute-done.1.other_in_ref
  56.7 12.4 %cells_step.1 = (bf16[32,64,1024]{2,1,0:T(8,128)(2,1)S(1)}, bf16[32,32,128]{2,1,0:T(8,128)(2,1)S(1)}, bf16[32,32,128]{2,1,0:T(8,128)(2,1)S(1)}, bf16[64,128]{1,0:T(8,128)(2,1)S(1)}) custom-call(s32[2]{0:T(128)S(1)} %pad_add_fusion.place.refs_0_, bf16[32,64,1024]{2,1,0:T(8,128)(2,1)S(1)} %get-tuple-element.16.field_ref, bf16[64,32,1024]{2,1,0:T(8,128)(2,1)S(1)} %bitcast.7, ...), custom_call_target="tpu_custom_call" | custom-call | tf_op jit(solution)/shard_map/cells_step/pallas_call | solution.py:382
  69.1 0.5 collective-permute-start.2
  69.6 1.2 collective-permute-done.2.refs_3_
  70.8 1.1 x_forward.3
  71.9 17.9 %all_to_all.22.sent_ref = bf16[64,40,128]{2,1,0:T(8,128)(2,1)S(1)} all-to-all(bf16[64,40,128]{2,1,0:T(8,128)(2,1)S(1)} %x_forward.3), channel_id=1, replica_groups=mesh['gx'=64,'gy'=2] {'gx'}, dimensions={0} | all-to-all | bytes 1310720 | tf_op jit(solution)/shard_map/all_to_all | solution.py:495
  89.8 1.0 mix_back.1
  90.8 17.0 %all_to_all.23.sent_ref = bf16[64,40,128]{2,1,0:T(8,128)(2,1)S(1)} all-to-all(bf16[64,40,128]{2,1,0:T(8,128)(2,1)S(1)} %get-tuple-element.24), channel_id=1, replica_groups=mesh['gx'=64,'gy'=2] {'gx'}, dimensions={0} | all-to-all | bytes 1310720 | tf_op jit(solution)/shard_map/all_to_all | solution.py:495
  107.8 1.4 %x_inverse.3.own_in_ref.own_tail_ref = bf16[34,32,128]{2,1,0:T(8,128)(2,1)S(1)} custom-call(s32[2]{0:T(128)S(1)} %pad_add_fusion.place.refs_0_, bf16[64,2,32,64]{3,2,1,0:T(8,128)(2,1)S(1)} %copy-done.3, bf16[64,40,128]{2,1,0:T(8,128)(2,1)S(1)} %all_to_all.23.sent_ref), custom_call_target="tpu_custom_call" | custom-call | tf_op jit(solution)/shard_map/x_inverse/pallas_call | solution.py:176
  109.1 3.2 %collective-permute-start.3 = (bf16[34,32,128]{2,1,0:T(8,128)(2,1)S(1)}, bf16[34,32,128]{2,1,0:T(8,128)(2,1)S(1)}, u32[]{:S(2)}, u32[]{:S(2)}) collective-permute-start(bf16[34,32,128]{2,1,0:T(8,128)(2,1)S(1)} %x_inverse.3.own_in_ref.own_tail_ref), channel_id=1, source_target_pairs={{0,1},{1,0},{2,3},{3,2},{4,5},{5,4},{6,7},{7,6},{8,9},{9,8},{10,11... | collective-permute-start | bytes 835592 | tf_op jit(solution)/shard_map/ppermute | solution.py:491
  112.4 2.1 %outer.1 = f32[32,64,128]{2,1,0:T(8,128)} custom-call(bf16[64,64]{1,0:T(8,128)(2,1)S(1)} %get-tuple-element.26.spectrum_ref, bf16[64,128]{1,0:T(8,128)(2,1)S(1)} %get-tuple-element.27.pair_ref), custom_call_target="tpu_custom_call" | custom-call | flops 33554432 | bytes 1048576 | tf_op jit(solution)/shard_map/outer/pallas_call | solution.py:284
  114.5 7.3 %last_step.1 = (bf16[64,32,1024]{2,1,0:T(8,128)(2,1)}, f32[64,64]{1,0:T(8,128)}) custom-call(s32[2]{0:T(128)S(1)} %pad_add_fusion.place.refs_0_, bf16[32,64,1024]{2,1,0:T(8,128)(2,1)S(1)} %get-tuple-element.20.slope_ref, bf16[34,32,128]{2,1,0:T(8,128)(2,1)S(1)} %x_inverse.3.own_in_ref.own_tail_ref, ...), custom_call_target="tpu_custom_call" | custom-call | tf_op jit(solution)/shard_map/last_step/pallas_call | solution.py:461
  (15 shorter events, 0.0 us)
Async XLA Ops:
  0.6 9.4 %copy-start = (bf16[64,2,64,32]{3,2,1,0:T(8,128)(2,1)S(1)}, bf16[64,2,64,32]{3,2,1,0:T(8,128)(2,1)}, u32[]{:S(2)}) copy-start(bf16[64,2,64,32]{3,2,1,0:T(8,128)(2,1)} %constant.18.clone.refs_1_) | copy-start | bytes 1572868
  0.7 2.3 %copy-start.2 = (bf16[1,64,32,1024]{3,2,1,0:T(8,128)(2,1)S(1)}, bf16[1,64,32,1024]{3,2,1,0:T(8,128)(2,1)}, u32[]{:S(2)}) copy-start(bf16[1,64,32,1024]{3,2,1,0:T(8,128)(2,1)} %param.8) | copy-start | bytes 12582916
  3.0 0.9 copy-start.6
  4.0 30.4 %copy-start.5 = (bf16[1,32,64,128]{3,2,1,0:T(8,128)(2,1)S(1)}, bf16[1,32,64,128]{3,2,1,0:T(8,128)(2,1)}, u32[]{:S(2)}) copy-start(bf16[1,32,64,128]{3,2,1,0:T(8,128)(2,1)} %param.11) | copy-start | bytes 1572868
  7.3 43.5 %copy-start.3 = (bf16[64,2,32,64]{3,2,1,0:T(8,128)(2,1)S(1)}, bf16[64,2,32,64]{3,2,1,0:T(8,128)(2,1)}, u32[]{:S(2)}) copy-start(bf16[64,2,32,64]{3,2,1,0:T(8,128)(2,1)} %constant.19.clone.phase_ref) | copy-start | bytes 1572868
  7.3 49.4 %copy-start.1 = (bf16[1,64,32,1024]{3,2,1,0:T(8,128)(2,1)S(1)}, bf16[1,64,32,1024]{3,2,1,0:T(8,128)(2,1)}, u32[]{:S(2)}) copy-start(bf16[1,64,32,1024]{3,2,1,0:T(8,128)(2,1)} %param.9) | copy-start | bytes 12582916
  7.3 49.4 %copy-start.4 = (bf16[256,1024]{1,0:T(8,128)(2,1)S(1)}, bf16[256,1024]{1,0:T(8,128)(2,1)}, u32[]{:S(2)}) copy-start(bf16[256,1024]{1,0:T(8,128)(2,1)} %constant.17.clone.back_ref) | copy-start | bytes 1572868
  7.4 49.4 %copy-start.7 = (bf16[64,64]{1,0:T(8,128)(2,1)S(1)}, bf16[64,64]{1,0:T(8,128)(2,1)}, u32[]{:S(2)}) copy-start(bf16[64,64]{1,0:T(8,128)(2,1)} %local_ref.3) | copy-start | bytes 24580
  7.4 2.7 %collective-permute-start = (bf16[32,32,128]{2,1,0:T(8,128)(2,1)S(1)}, bf16[32,32,128]{2,1,0:T(8,128)(2,1)S(1)}, u32[]{:S(2)}, u32[]{:S(2)}) collective-permute-start(bf16[32,32,128]{2,1,0:T(8,128)(2,1)S(1)} %get-tuple-element.18), channel_id=1, source_target_pairs={{0,1},{1,0},{2,3},{3,2},{4,5},{5,4},{6,7},{7,6},{8,9},{9,8},{10,11... | collective-permute-start | bytes 786440 | tf_op jit(solution)/shard_map/ppermute | solution.py:491
  52.2 4.5 %collective-permute-start.1 = (bf16[32,32,128]{2,1,0:T(8,128)(2,1)S(1)}, bf16[32,32,128]{2,1,0:T(8,128)(2,1)S(1)}, u32[]{:S(2)}, u32[]{:S(2)}) collective-permute-start(bf16[32,32,128]{2,1,0:T(8,128)(2,1)S(1)} %x_inverse.2.own_in_ref), channel_id=1, source_target_pairs={{0,1},{1,0},{2,3},{3,2},{4,5},{5,4},{6,7},{7,6},{8,9},{9,8},{10,11... | collective-permute-start | bytes 786440 | tf_op jit(solution)/shard_map/ppermute | solution.py:491
  69.1 1.6 %collective-permute-start.2 = (bf16[32,32,128]{2,1,0:T(8,128)(2,1)S(1)}, bf16[32,32,128]{2,1,0:T(8,128)(2,1)S(1)}, u32[]{:S(2)}, u32[]{:S(2)}) collective-permute-start(bf16[32,32,128]{2,1,0:T(8,128)(2,1)S(1)} %get-tuple-element.22), channel_id=1, source_target_pairs={{0,1},{1,0},{2,3},{3,2},{4,5},{5,4},{6,7},{7,6},{8,9},{9,8},{10,11... | collective-permute-start | bytes 786440 | tf_op jit(solution)/shard_map/ppermute | solution.py:491
  109.1 5.4 %collective-permute-start.3 = (bf16[34,32,128]{2,1,0:T(8,128)(2,1)S(1)}, bf16[34,32,128]{2,1,0:T(8,128)(2,1)S(1)}, u32[]{:S(2)}, u32[]{:S(2)}) collective-permute-start(bf16[34,32,128]{2,1,0:T(8,128)(2,1)S(1)} %x_inverse.3.own_in_ref.own_tail_ref), channel_id=1, source_target_pairs={{0,1},{1,0},{2,3},{3,2},{4,5},{5,4},{6,7},{7,6},{8,9},{9,8},{10,11... | collective-permute-start | bytes 835592 | tf_op jit(solution)/shard_map/ppermute | solution.py:491
where the time goes:
time: 122 us
  blocking collectives  73.6 us (60%)
  Pallas kernels  32.1 us (26%)
  starting transfers between devices  8.58 us (7%)
  waiting for transfers between devices  3.49 us (3%)
  local copies, waits for them, and re-layouts  3.31 us (3%)
    all_to_all x4, blocking collectives, exchange(): return lax.all_to_all(rows, 'gx', 0, 0, tiled=True)  73.6 us
    pallas_call x1, Pallas kernels, cells_step(): pl.pallas_call(cells_kernel, grid_spec=pltpu.PrefetchScalarGridSpec(num_s...  12.4 us
    ppermute x4, starting transfers between devices, swap_cores(): return lax.ppermute(values, 'gy', [(0, 1), (1, 0)])  8.58 us
    pallas_call x1, Pallas kernels, last_step(): pl.pallas_call(last_kernel, grid_spec=pltpu.PrefetchScalarGridSpec(num_sc...  7.34 us
    ppermute x4, waiting for transfers between devices, swap_cores(): return lax.ppermute(values, 'gy', [(0, 1), (1, 0)])  3.49 us
    pallas_call x1, Pallas kernels, y_forward(): pl.pallas_call(y_forward_kernel, grid_spec=pltpu.PrefetchScalarGridSpec(n...  3.31 us
    unnamed x16, local copies, waits for them, and re-layouts  3.31 us
    pallas_call x2, Pallas kernels, x_inverse(): pl.pallas_call(x_inverse_kernel, grid_spec=pltpu.PrefetchScalarGridSpec(n...  2.72 us
  transfers between devices with their start and end apart: 4, of which 3 were waited for; matrix products, arithmetic and copies ran while one was open for 0% of the time, Pallas kernels for 2%

commit v1 on v0

v1 whole, which is shorter than its diff:
```python
import math

import jax
import jax.experimental.pallas as pl
import jax.experimental.pallas.tpu as pltpu
import jax.numpy as jnp
import numpy as np
from jax import lax
from jax.sharding import PartitionSpec as P

NX = 2048
NY = 2048
C = 64
MX = 64
MY = 64
SHARDS = 64
XC = 32
YC = 1024
YB = 256
YO = 512
TWO_PI = 2.0 * math.pi
ROOT_HALF = 1.0 / math.sqrt(2.0)
ROOT_TWO_PI = 1.0 / math.sqrt(2.0 * math.pi)
FORWARD = 1.0 / math.sqrt(NX * NY)
INVERSE = 1.0 / math.sqrt(MX * MY)
GAMMA = math.sqrt(MX * MY / (NX * NY))
BF = jnp.bfloat16
F32 = jnp.float32
RIDER = 8


def tables():
    angle = (np.arange(YC)[:, None] * np.arange(MY)[None, :] % NY) * (TWO_PI / NY)
    pair = np.stack([np.cos(angle), -np.sin(angle)], axis=1).reshape(YC, 2, 2, 32)
    forth = np.transpose(pair, (0, 2, 1, 3)).reshape(YC, 128)
    modes = np.arange(MX)
    frequency = np.where(modes < MX // 2, modes, modes + NX - MX)
    xangle = (frequency[:, None] * np.arange(XC)[None, :] % NX) * (TWO_PI / NX)
    phase = np.stack([np.cos(xangle), np.sin(xangle)])
    origin = (modes[:, None] * np.arange(SHARDS)[None, :] % SHARDS) * (TWO_PI / SHARDS)
    return forth, forth.T, phase, np.stack([np.cos(origin), np.sin(origin)])


def dot(a, b, dims=((1,), (0,))):
    return lax.dot_general(a, b, (dims, ((), ())), preferred_element_type=F32)


VMEM = pl.BlockSpec(memory_space=pltpu.VMEM)
SMEM = pl.BlockSpec(memory_space=pltpu.SMEM)


def iota(shape, axis):
    return lax.broadcasted_iota(jnp.int32, shape, axis)


def turn(values, sign):
    lane = iota(values.shape, 1)
    first = lane % 64 < 32
    return jnp.where(first, sign * pltpu.roll(values, 96, 1), -sign * pltpu.roll(values, 32, 1))


def parity(core, shape):
    return jnp.where((iota(shape, len(shape) - 1) % 2) * core == 1, -1.0, 1.0).astype(F32)


def split_halves(parts, cells, groups, core):
    rows = cells * groups * 8
    blocks = parts.reshape(cells * groups, 2, 8, 128)
    first = blocks[:, 0].reshape(rows, 128)
    second = blocks[:, 1].reshape(rows, 128)
    low = iota((rows, 128), 1) < 64
    sign = parity(core, (rows, 128))
    half_a = jnp.where(low, first, pltpu.roll(second, 64, 1)) * sign
    half_b = jnp.where(low, pltpu.roll(first, 64, 1), second) * sign
    own = jnp.where(core == 0, half_a, half_b)
    other = jnp.where(core == 0, half_b, half_a)
    shape = (cells, groups * 8, 128)
    return own.reshape(shape).astype(BF), other.reshape(shape).astype(BF)


def y_forward_kernel(place, field_ref, forth_ref, cells_ref, own_ref, other_ref, held, arrived):
    def copy(k):
        group, half = k // 2, k % 2
        channels = pl.ds(pl.multiple_of(32 * group, 32), 32)
        cells = pl.ds(pl.multiple_of(16 * half, 16), 16)
        return pltpu.make_async_copy(field_ref.at[channels, cells], held.at[k], arrived.at[k])

    for k in range(4):
        copy(k).start()

    @pl.loop(0, 4)
    def _(k):
        group, half = k // 2, k % 2
        copy(k).wait()
        rows = jnp.swapaxes(held[k], 0, 1)
        cells = pl.ds(pl.multiple_of(16 * half, 16), 16)
        cells_ref[cells, pl.ds(pl.multiple_of(32 * group, 32), 32), :] = rows
        parts = dot(rows.reshape(16 * 32, YC), forth_ref[...])
        own, other = split_halves(parts, 16, 2, place[1])
        channels = pl.ds(pl.multiple_of(16 * group, 16), 16)
        own_ref[cells, channels, :] = own
        other_ref[cells, channels, :] = other


def y_forward(place, field, forth):
    return pl.pallas_call(
        y_forward_kernel,
        in_specs=[SMEM, pl.BlockSpec(memory_space=pltpu.HBM), VMEM],
        out_specs=[VMEM, VMEM, VMEM],
        out_shape=[
            pltpu.VMEM((XC, C, YC), BF),
            pltpu.VMEM((XC, 32, 128), BF),
            pltpu.VMEM((XC, 32, 128), BF),
        ],
        scratch_shapes=[pltpu.VMEM((4, 32, 16, YC), BF), pltpu.SemaphoreType.DMA((4,))],
        compiler_params=pltpu.CompilerParams(vmem_limit_bytes=16 << 20),
        name="y_forward",
    )(place, pltpu.with_memory_space_constraint(field, pltpu.HBM), forth)


def rotated(phase_ref, origin_ref, shard, axis):
    at = iota((MX, SHARDS), 1 - axis) == shard
    cosine, sine = [
        jnp.sum(jnp.where(at, origin_ref[q], 0.0), axis=1 - axis, keepdims=True) for q in range(2)
    ]
    real, imag = phase_ref[0], phase_ref[1]
    return (cosine * real - sine * imag).astype(BF), (sine * real + cosine * imag).astype(BF)


def x_forward_kernel(scale, place, phase_ref, origin_ref, own_ref, other_ref, *rest):
    out_ref = rest[-1]
    total = own_ref[...].astype(F32) + other_ref[...].astype(F32)
    widen = (iota((XC, 256), 1) // 8 == iota((XC, 256), 0)).astype(BF)
    keep = iota((1, 8, 256), 2) % 8 == iota((1, 8, 256), 1)
    left = []
    for table in rotated(phase_ref, origin_ref, place[0], 0):
        wide = dot(table, widen)
        left.append(jnp.where(keep, wide[:, None, :], 0.0).reshape(512, 256).astype(BF))
    left = jnp.concatenate(left, axis=1)
    for g in range(2):
        right = []
        for s in range(2):
            rows = total[:, 16 * g + 8 * s : 16 * g + 8 * s + 8].reshape(256, 128)
            right.append(jnp.concatenate([rows, turn(rows, 1.0)], axis=0))
        modes = dot(left, jnp.concatenate(right, axis=1).astype(BF)) * scale
        both = [modes[:, 128 * s : 128 * s + 128].reshape(64, 8, 128) for s in range(2)]
        out_ref[:, 16 * g : 16 * g + 16, :] = jnp.concatenate(both, axis=1).astype(BF)
    if len(rest) == 2:
        rider = rest[0][...].astype(F32)
        out_ref[:, 32:, :] = jnp.broadcast_to(rider[:, None, :], (64, RIDER, 128)).astype(BF)


def x_forward(place, phase, origin, own, other, scale, rider=None):
    rows = 32 if rider is None else 32 + RIDER
    operands = [own, other] + ([] if rider is None else [rider])
    return pl.pallas_call(
        lambda *refs: x_forward_kernel(scale, *refs),
        in_specs=[SMEM, VMEM, VMEM] + [VMEM] * len(operands),
        out_specs=VMEM,
        out_shape=pltpu.VMEM((SHARDS, rows, 128), BF),
        compiler_params=pltpu.CompilerParams(vmem_limit_bytes=16 << 20),
        name="x_forward",
    )(place, phase, origin, *operands)


def x_inverse_kernel(place, phase_ref, origin_ref, sent_ref, inner_ref):
    widen = (iota((MX, 512), 1) // 8 == iota((MX, 512), 0)).astype(BF)
    keep = iota((1, 8, 512), 2) % 8 == iota((1, 8, 512), 1)
    left = []
    for table in rotated(phase_ref, origin_ref, place[0], 1):
        wide = dot(table, widen)
        left.append(jnp.where(keep, wide[:, None, :], 0.0).reshape(256, 512).astype(BF))
    left = jnp.concatenate(left, axis=0)
    for g in range(2):
        rows = sent_ref[:, 16 * g : 16 * g + 16, :].astype(F32)
        right = [rows[:, 8 * s : 8 * s + 8].reshape(512, 128) for s in range(2)]
        both = dot(left, jnp.concatenate(right, axis=1).astype(BF))
        inner = []
        for s in range(2):
            piece = both[:, 128 * s : 128 * s + 128]
            inner.append((piece[:256] + turn(piece[256:], -1.0)).reshape(XC, 8, 128))
        inner_ref[:XC, 16 * g : 16 * g + 16, :] = jnp.concatenate(inner, axis=1).astype(BF)
    if sent_ref.shape[1] > 32:
        rider = sent_ref[:, 32:, :].astype(F32)[:, 0, :]
        inner_ref[XC:, :, :] = rider.reshape(2, 32, 128).astype(BF)


def x_inverse(place, phase, origin, sent):
    cells = XC if sent.shape[1] == 32 else XC + 2
    return pl.pallas_call(
        x_inverse_kernel,
        in_specs=[SMEM, VMEM, VMEM, VMEM],
        out_specs=VMEM,
        out_shape=pltpu.VMEM((cells, 32, 128), BF),
        compiler_params=pltpu.CompilerParams(vmem_limit_bytes=16 << 20),
        name="x_inverse",
    )(place, phase, origin, sent)


def pick(b):
    r = iota((32, C), 0)
    return (iota((32, C), 1) == (r // 8) * 16 + b * 8 + r % 8).astype(BF)


def modes_of(rows):
    flipped = rows.T.astype(BF)
    return (dot(flipped[:64], pick(0)) + dot(flipped[64:], pick(1))).astype(BF)


def rows_of(real, imag):
    blocks = [dot(pick(b), part, ((1,), (1,))) for b in range(2) for part in (real, imag)]
    return jnp.concatenate(blocks, axis=1)


def own_mode(shape):
    return iota(shape, 1) // C == iota(shape, 0) % 32


def mix_kernel(sent_ref, weight_ref, out_ref, spectrum_ref):
    spectrum = modes_of(jnp.sum(sent_ref[...].astype(F32), axis=0))
    spectrum_ref[...] = spectrum
    pair = spectrum.astype(F32)
    pair = jnp.concatenate([pair, pair], axis=1)
    wide = jnp.concatenate([pair] * 16, axis=1)
    wide = jnp.where(own_mode(wide.shape), wide, 0.0).astype(BF)
    product = dot(wide, weight_ref[...].reshape(32 * C, 128))
    lane = iota((32, 128), 1)
    mixed = product[:32] + jnp.where(lane < 64, -1.0, 1.0) * pltpu.roll(product[32:], 64, 1)
    mixed = mixed.astype(BF)
    rows = rows_of(mixed[:, :64], mixed[:, 64:])
    out_ref[...] = jnp.broadcast_to(rows[None], (SHARDS, 32, 128)).astype(BF)


def mix(sent, weights):
    return pl.pallas_call(
        mix_kernel,
        out_shape=[
            jax.ShapeDtypeStruct((SHARDS, 32, 128), BF),
            jax.ShapeDtypeStruct((64, C), BF),
        ],
        compiler_params=pltpu.CompilerParams(vmem_limit_bytes=20 << 20),
        name="mix",
    )(sent, weights)


def mix_back_kernel(sent_ref, weight_ref, out_ref, pair_ref):
    total = jnp.sum(sent_ref[...].astype(F32), axis=0)
    modes = modes_of(total[:32]).astype(F32)
    real, imag = modes[:32], modes[32:]
    left = jnp.concatenate([real, imag], axis=1)
    right = jnp.concatenate([imag, -real], axis=1)
    pair = jnp.concatenate([left, right], axis=0).astype(BF)
    pair_ref[...] = pair
    product = dot(pair, weight_ref[...].reshape(32 * C, 128), ((1,), (1,)))
    product = jnp.where(own_mode(product.shape), product, 0.0)
    folded = product[:, :128]
    for k in range(1, 16):
        folded = folded + product[:, 128 * k : 128 * k + 128]
    folded = (folded + pltpu.roll(folded, 64, 1))[:, :64].astype(BF)
    rows = rows_of(folded[:32], folded[32:])
    rider = total[32:]
    rider = rider + pltpu.roll(rider, 64, 1)
    high = rider.astype(BF).astype(F32)
    rider = jnp.where(iota(rider.shape, 1) < 64, high, rider - high)
    rows = jnp.concatenate([rows, rider], axis=0)
    out_ref[...] = jnp.broadcast_to(rows[None], (SHARDS, 32 + RIDER, 128)).astype(BF)


def mix_back(sent, weights):
    return pl.pallas_call(
        mix_back_kernel,
        out_shape=[
            jax.ShapeDtypeStruct((SHARDS, 32 + RIDER, 128), BF),
            jax.ShapeDtypeStruct((64, 128), BF),
        ],
        compiler_params=pltpu.CompilerParams(vmem_limit_bytes=20 << 20),
        name="mix_back",
    )(sent, weights)


def outer_kernel(spectrum_ref, pair_ref, out_ref):
    flipped = spectrum_ref[...].astype(F32).T
    tall = jnp.concatenate([flipped] * 8, axis=0)
    shape = tall.shape
    keep = iota(shape, 1) % 32 == iota(shape, 0) // C + 8 * pl.program_id(0)
    tall = jnp.where(keep, tall, 0.0).astype(BF)
    out_ref[...] = (dot(tall, pair_ref[...]) * GAMMA).reshape(8, C, 128)


def outer(spectrum, pair):
    return pl.pallas_call(
        outer_kernel,
        grid=(4,),
        in_specs=[pl.BlockSpec((64, C), lambda i: (0, 0)), pl.BlockSpec((64, 128), lambda i: (0, 0))],
        out_specs=pl.BlockSpec((8, C, 128), lambda i: (i, 0, 0)),
        out_shape=jax.ShapeDtypeStruct((32, C, 128), F32),
        compiler_params=pltpu.CompilerParams(vmem_limit_bytes=20 << 20),
        cost_estimate=pl.CostEstimate(flops=2 * 2048 * 64 * 128, bytes_accessed=1 << 20, transcendentals=0),
        name="outer",
    )(spectrum, pair)


def gelu_slope(values):
    return (
        0.5 * (1.0 + lax.erf(values * ROOT_HALF))
        + values * jnp.exp(-0.5 * values * values) * ROOT_TWO_PI
    )


def block_diagonal(square):
    wide = jnp.concatenate([square, square], axis=1)
    full = jnp.concatenate([wide, wide], axis=0)
    return jnp.where(iota(full.shape, 0) // C == iota(full.shape, 1) // C, full, 0.0)


def inner_rows(core, scale, own_ref, other_ref, rows_ref):
    own = own_ref[:XC].astype(F32).reshape(XC * 32, 128)
    other = other_ref[:XC].astype(F32).reshape(XC * 32, 128)
    sign = parity(core, own.shape) * scale
    half_a = jnp.where(core == 0, own, other) * sign
    half_b = jnp.where(core == 0, other, own) * sign
    low = iota(own.shape, 1) < 64
    first = jnp.where(low, half_a, pltpu.roll(half_b, 64, 1)).reshape(XC * 4, 8, 128)
    second = jnp.where(low, pltpu.roll(half_a, 64, 1), half_b).reshape(XC * 4, 8, 128)
    rows_ref[...] = jnp.stack([first, second], axis=1).reshape(XC * C, 128).astype(BF)


def mixed_cells(diagonal, inner, cells, back, start):
    pieces = []
    for k in range(cells.shape[0] // 128):
        rows = inner[start + 128 * k : start + 128 * k + 128, :]
        left = jnp.concatenate([diagonal, rows], axis=1)
        right = jnp.concatenate([cells[128 * k : 128 * k + 128], back], axis=0)
        pieces.append(dot(left, right))
    return jnp.concatenate(pieces, axis=0)


def cells_kernel(
    place,
    field_ref,
    cotangent_ref,
    own_in_ref,
    other_in_ref,
    local_ref,
    forth_ref,
    back_ref,
    slope_ref,
    own_ref,
    other_ref,
    weight_ref,
    inner,
):
    diagonal = block_diagonal(local_ref[...].astype(F32)).T.astype(BF)
    inner_rows(place[1], INVERSE, own_in_ref, other_in_ref, inner)
    products = jnp.zeros((256, 256), F32)
    tiles = [(half, y, g) for half in range(2) for y in range(YC // YB) for g in range(4)]
    flipped, ready, made = {}, {}, {}
    sums = {}

    def place_of(tile):
        half, y, g = tile
        cells = slice(16 * half + 4 * g, 16 * half + 4 * g + 4)
        return cells, slice(C * cells.start, C * cells.stop), slice(YB * y, YB * y + YB)

    def begin(tile):
        half, y, g = tile
        cells, rows, columns = place_of(tile)
        if g == 0:
            flipped[half, y] = jnp.swapaxes(cotangent_ref[:, 16 * half : 16 * half + 16, columns], 0, 1)
        field = field_ref[cells, :, columns].reshape(256, YB)
        ready[tile] = mixed_cells(diagonal, inner, field, back_ref[:, columns], rows.start)

    def bend(tile):
        half, y, g = tile
        cells, rows, columns = place_of(tile)
        upper = flipped[half, y][4 * g : 4 * g + 4].reshape(256, YB).astype(F32)
        slope = (upper * gelu_slope(ready.pop(tile))).astype(BF)
        slope_ref[cells, :, columns] = slope.reshape(4, C, YB)
        made[tile] = slope

    def end(tile, products):
        half, y, g = tile
        cells, rows, columns = place_of(tile)
        slope = made.pop(tile)
        field = field_ref[cells, :, columns].reshape(256, YB)
        part = dot(slope, forth_ref[columns, :])
        sums[half, g] = part if y == 0 else sums[half, g] + part
        return products + dot(field, slope, ((1,), (1,)))

    for t in range(len(tiles) + 2):
        if t < len(tiles):
            begin(tiles[t])
        if t >= 2:
            products = end(tiles[t - 2], products)
        if 1 <= t <= len(tiles):
            bend(tiles[t - 1])
    for half in range(2):
        cells = slice(16 * half, 16 * half + 16)
        parts = jnp.concatenate([sums[half, g] for g in range(4)], axis=0)
        own_ref[cells], other_ref[cells] = split_halves(parts, 16, 4, place[1])
    total = products[:64, :128] + pltpu.roll(products[64:128, :128], 64, 1)
    total = total + products[128:192, 128:] + pltpu.roll(products[192:, 128:], 64, 1)
    high = total.astype(BF).astype(F32)
    low = pltpu.roll(total - high, 64, 1)
    weight_ref[...] = jnp.where(iota((64, 128), 1) < 64, high, low).astype(BF)


def cells_step(place, cells, cotangent, own, other, local_weight, forth, back):
    return pl.pallas_call(
        cells_kernel,
        in_specs=[SMEM] + [VMEM] * 7,
        out_specs=[VMEM] * 4,
        out_shape=[
            pltpu.VMEM((XC, C, YC), BF),
            pltpu.VMEM((XC, 32, 128), BF),
            pltpu.VMEM((XC, 32, 128), BF),
            pltpu.VMEM((64, 128), BF),
        ],
        scratch_shapes=[pltpu.VMEM((XC * C, 128), BF)],
        compiler_params=pltpu.CompilerParams(vmem_limit_bytes=24 << 20),
        name="cells_step",
    )(place, cells, cotangent, own, other, local_weight, forth, back)


def last_kernel(
    place,
    slope_ref,
    own_in_ref,
    other_in_ref,
    local_ref,
    back_ref,
    out_ref,
    grad_local_ref,
    inner,
    staged,
    sent,
):
    total = own_in_ref[XC:].astype(F32).reshape(64, 128)
    total = total + pltpu.roll(total, 64, 1)
    more = other_in_ref[XC:].astype(F32).reshape(64, 128)
    more = more + pltpu.roll(more, 64, 1)
    grad_local_ref[...] = (total + more)[:, :64] * FORWARD
    diagonal = block_diagonal(local_ref[...].astype(F32)).astype(BF)
    inner_rows(place[1], FORWARD, own_in_ref, other_in_ref, inner)
    chunks = [(half, y) for half in range(2) for y in range(YC // YO)]

    def copy(k):
        half, y = chunks[k]
        target = out_ref.at[:, 16 * half : 16 * half + 16, YO * y : YO * y + YO]
        return pltpu.make_async_copy(staged.at[k], target, sent.at[k])

    def finish(k, pieces):
        staged[k] = jnp.swapaxes(jnp.concatenate(pieces, axis=0), 0, 1)
        copy(k).start()

    ready = None
    for k, (half, y) in enumerate(chunks):
        columns = slice(YO * y, YO * y + YO)
        pieces = []
        for g in range(4):
            cells = slice(16 * half + 4 * g, 16 * half + 4 * g + 4)
            slope = slope_ref[cells, :, columns].reshape(256, YO)
            total = mixed_cells(diagonal, inner, slope, back_ref[:, columns], C * cells.start)
            pieces.append(total.astype(BF).reshape(4, C, YO))
            if g == 0 and ready is not None:
                finish(k - 1, ready)
        ready = pieces
    finish(len(chunks) - 1, ready)
    for k in range(len(chunks)):
        copy(k).wait()


def last_step(place, slope, own, other, local_weight, back):
    number = 2 * (YC // YO)
    return pl.pallas_call(
        last_kernel,
        in_specs=[SMEM] + [VMEM] * 5,
        out_specs=[pl.BlockSpec(memory_space=pltpu.HBM), VMEM],
        scratch_shapes=[
            pltpu.VMEM((XC * C, 128), BF),
            pltpu.VMEM((number, C, 16, YO), BF),
            pltpu.SemaphoreType.DMA((number,)),
        ],
        out_shape=[
            jax.ShapeDtypeStruct((C, XC, YC), BF),
            jax.ShapeDtypeStruct((C, C), F32),
        ],
        compiler_params=pltpu.CompilerParams(vmem_limit_bytes=24 << 20),
        name="last_step",
    )(place, slope, own, other, local_weight, back)


def swap_cores(values):
    return lax.ppermute(values, "gy", [(0, 1), (1, 0)])


def exchange(rows):
    return lax.all_to_all(rows, "gx", 0, 0, tiled=True)


def on_device(field, cotangent, local_weight, spectral_weight):
    forth, back, phase, origin = tables()
    forth, back = [jnp.asarray(t.astype(np.float32), BF) for t in (forth, back)]
    phase_back = jnp.asarray(np.transpose(phase, (0, 2, 1)), F32)
    phase, origin = [jnp.asarray(t, F32) for t in (phase, origin)]
    place = jnp.stack([lax.axis_index("gx"), lax.axis_index("gy")]).astype(jnp.int32)
    weights = spectral_weight[0]

    cells, own, other = y_forward(place, field[0], forth)
    sent = exchange(x_forward(place, phase, origin, own, swap_cores(other), FORWARD))
    copies, spectrum = mix(sent, weights)
    inner = x_inverse(place, phase_back, origin, exchange(copies))
    slope, own, other, rider = cells_step(
        place, cells, cotangent[0], inner, swap_cores(inner), local_weight, forth, back
    )
    sent = exchange(x_forward(place, phase, origin, own, swap_cores(other), INVERSE, rider))
    copies, pair = mix_back(sent, weights)
    inner = x_inverse(place, phase_back, origin, exchange(copies))
    grad_spectral = outer(spectrum, pair)
    grad_field, grad_local = last_step(place, slope, inner, swap_cores(inner), local_weight, back)
    return (grad_field[None], grad_spectral[None], grad_local)


def solution(mesh):
    placed = (P(None, None, "gx", "gy"), P(None, None, "gx", "gy"), P(), P("gx", "gy", None, None))
    return jax.shard_map(
        on_device,
        mesh=mesh,
        in_specs=placed,
        out_specs=(P(None, None, "gx", "gy"), P("gx", "gy", None, None), P()),
        check_vma=False,
    )
```

time: 122 us -> 116 us (0.951)
  Pallas kernels: 32.1 us -> 26.1 us
    pallas_call x7, Pallas kernels: 28 us -> 22.1 us  [the longest x1 7.7 us: cells_step(): pl.pallas_call(cells_kernel, in_specs=[SMEM] + [VMEM] * 7, out_specs=[VME...]
    unnamed x16 -> x22, local copies, waits for them, and re-layouts: 3.31 us -> 2.71 us
where the time goes in v1:
time: 116 us
  blocking collectives  73.6 us (63%)
  Pallas kernels  26.1 us (22%)
  starting transfers between devices  8.76 us (8%)
  waiting for transfers between devices  3.49 us (3%)
  local copies, waits for them, and re-layouts  2.71 us (2%)
    all_to_all x4, blocking collectives, exchange(): return lax.all_to_all(rows, 'gx', 0, 0, tiled=True)  73.6 us
    ppermute x4, starting transfers between devices, swap_cores(): return lax.ppermute(values, 'gy', [(0, 1), (1, 0)])  8.76 us
    pallas_call x1, Pallas kernels, cells_step(): pl.pallas_call(cells_kernel, in_specs=[SMEM] + [VMEM] * 7, out_specs=[VME...  7.7 us
    pallas_call x1, Pallas kernels, last_step(): pl.pallas_call(last_kernel, in_specs=[SMEM] + [VMEM] * 5, out_specs=[pl.B...  4.94 us
    pallas_call x1, Pallas kernels, y_forward(): pl.pallas_call(y_forward_kernel, in_specs=[SMEM, pl.BlockSpec(memory_spac...  4.29 us
    ppermute x4, waiting for transfers between devices, swap_cores(): return lax.ppermute(values, 'gy', [(0, 1), (1, 0)])  3.49 us
    pallas_call x2, Pallas kernels, x_inverse(): pl.pallas_call(x_inverse_kernel, in_specs=[SMEM, VMEM, VMEM, VMEM], out_s...  2.76 us
    unnamed x22, local copies, waits for them, and re-layouts  2.71 us
  transfers between devices with their start and end apart: 4, of which 3 were waited for; matrix products, arithmetic and copies ran while one was open for 0% of the time, Pallas kernels for 2%

profile of v1, /device:TPU:1, one launch (start us, length us, event | category | flops | bytes accessed | tf_op | source)
XLA Modules:
  0.0 115.6 jit_solution(11421887405935428982)
XLA Ops:
  0.7 1.0 copy-done.2
  1.7 4.3 %y_forward.1 = (bf16[32,64,1024]{2,1,0:T(8,128)(2,1)S(1)}, bf16[32,32,128]{2,1,0:T(8,128)(2,1)S(1)}, bf16[32,32,128]{2,1,0:T(8,128)(2,1)S(1)}) custom-call(s32[2]{0:T(128)S(1)} %pad_add_fusion.place.refs_0_, bf16[64,32,1024]{2,1,0:T(8,128)(2,1)} %bitcast.10, bf16[1024,128]{1,0:T(8,128)(2,1)S(1)} %copy-done.2), custom_call_target="tpu_custom_call" | custom-call | tf_op jit(solution)/shard_map/y_forward/pallas_call | solution.py:106
  6.0 1.5 %collective-permute-start = (bf16[32,32,128]{2,1,0:T(8,128)(2,1)S(1)}, bf16[32,32,128]{2,1,0:T(8,128)(2,1)S(1)}, u32[]{:S(2)}, u32[]{:S(2)}) collective-permute-start(bf16[32,32,128]{2,1,0:T(8,128)(2,1)S(1)} %get-tuple-element.18), channel_id=1, source_target_pairs={{0,1},{1,0},{2,3},{3,2},{4,5},{5,4},{6,7},{7,6},{8,9},{9,8},{10,11... | collective-permute-start | bytes 786440 | tf_op jit(solution)/shard_map/ppermute | solution.py:494
  7.5 1.2 %collective-permute-done.refs_4_ = bf16[32,32,128]{2,1,0:T(8,128)(2,1)S(1)} collective-permute-done((bf16[32,32,128]{2,1,0:T(8,128)(2,1)S(1)}, bf16[32,32,128]{2,1,0:T(8,128)(2,1)S(1)}, u32[]{:S(2)}, u32[]{:S(2)}) %collective-permute-start) | collective-permute-done | bytes 262176 | tf_op jit(solution)/shard_map/ppermute | solution.py:494
  8.7 0.8 copy-done.4
  9.5 0.8 copy-done.7
  10.4 1.2 %x_forward.2 = bf16[64,32,128]{2,1,0:T(8,128)(2,1)S(1)} custom-call(s32[2]{0:T(128)S(1)} %pad_add_fusion.place.refs_0_, f32[2,64,32]{2,1,0:T(8,128)S(1)} %copy-done.7, f32[2,64,64]{2,1,0:T(8,128)S(1)} %copy-done.4, bf16[32,32,128]{2,1,0:T(8,128)(2,1)S(1)} %get-tuple-element.17.refs_3_, bf16[32,32,128]{2,1,0:T(8,128)(2,1)S(1)} %collective-permute-done.refs_4_), custom_call_target="tpu_custom_call" | custom-call | tf_op jit(solution)/shard_map/x_forward/pallas_call | solution.py:156
  11.6 23.2 %all_to_all.20.sent_ref = bf16[64,32,128]{2,1,0:T(8,128)(2,1)S(1)} all-to-all(bf16[64,32,128]{2,1,0:T(8,128)(2,1)S(1)} %x_forward.2), channel_id=1, replica_groups=mesh['gx'=64,'gy'=2] {'gx'}, dimensions={0} | all-to-all | bytes 1048576 | tf_op jit(solution)/shard_map/all_to_all | solution.py:498
  34.8 1.0 mix.1
  35.8 15.4 %all_to_all.21.sent_ref = bf16[64,32,128]{2,1,0:T(8,128)(2,1)S(1)} all-to-all(bf16[64,32,128]{2,1,0:T(8,128)(2,1)S(1)} %get-tuple-element.19), channel_id=1, replica_groups=mesh['gx'=64,'gy'=2] {'gx'}, dimensions={0} | all-to-all | bytes 1048576 | tf_op jit(solution)/shard_map/all_to_all | solution.py:498
  51.2 1.4 %x_inverse.2.own_in_ref = bf16[32,32,128]{2,1,0:T(8,128)(2,1)S(1)} custom-call(s32[2]{0:T(128)S(1)} %pad_add_fusion.place.refs_0_, f32[2,32,64]{2,1,0:T(8,128)S(1)} %copy-done.9, f32[2,64,64]{2,1,0:T(8,128)S(1)} %copy-done.5, bf16[64,32,128]{2,1,0:T(8,128)(2,1)S(1)} %all_to_all.21.sent_ref), custom_call_target="tpu_custom_call" | custom-call | tf_op jit(solution)/shard_map/x_inverse/pallas_call | solution.py:190
  52.6 3.4 %collective-permute-start.1 = (bf16[32,32,128]{2,1,0:T(8,128)(2,1)S(1)}, bf16[32,32,128]{2,1,0:T(8,128)(2,1)S(1)}, u32[]{:S(2)}, u32[]{:S(2)}) collective-permute-start(bf16[32,32,128]{2,1,0:T(8,128)(2,1)S(1)} %x_inverse.2.own_in_ref), channel_id=1, source_target_pairs={{0,1},{1,0},{2,3},{3,2},{4,5},{5,4},{6,7},{7,6},{8,9},{9,8},{10,11... | collective-permute-start | bytes 786440 | tf_op jit(solution)/shard_map/ppermute | solution.py:494
  56.0 1.2 %collective-permute-done.1.other_in_ref = bf16[32,32,128]{2,1,0:T(8,128)(2,1)S(1)} collective-permute-done((bf16[32,32,128]{2,1,0:T(8,128)(2,1)S(1)}, bf16[32,32,128]{2,1,0:T(8,128)(2,1)S(1)}, u32[]{:S(2)}, u32[]{:S(2)}) %collective-permute-start.1) | collective-permute-done | bytes 262176 | tf_op jit(solution)/shard_map/ppermute | solution.py:494
  57.2 7.7 %cells_step.1 = (bf16[32,64,1024]{2,1,0:T(8,128)(2,1)S(1)}, bf16[32,32,128]{2,1,0:T(8,128)(2,1)S(1)}, bf16[32,32,128]{2,1,0:T(8,128)(2,1)S(1)}, bf16[64,128]{1,0:T(8,128)(2,1)S(1)}) custom-call(s32[2]{0:T(128)S(1)} %pad_add_fusion.place.refs_0_, bf16[32,64,1024]{2,1,0:T(8,128)(2,1)S(1)} %get-tuple-element.16.field_ref, bf16[64,32,1024]{2,1,0:T(8,128)(2,1)S(1)} %bitcast.7, ...), custom_call_target="tpu_custom_call" | custom-call | tf_op jit(solution)/shard_map/cells_step/pallas_call | solution.py:409
  64.9 0.6 collective-permute-start.2
  65.5 1.2 %collective-permute-done.2.refs_4_ = bf16[32,32,128]{2,1,0:T(8,128)(2,1)S(1)} collective-permute-done((bf16[32,32,128]{2,1,0:T(8,128)(2,1)S(1)}, bf16[32,32,128]{2,1,0:T(8,128)(2,1)S(1)}, u32[]{:S(2)}, u32[]{:S(2)}) %collective-permute-start.2) | collective-permute-done | bytes 262176 | tf_op jit(solution)/shard_map/ppermute | solution.py:494
  66.7 1.2 %x_forward.3 = bf16[64,40,128]{2,1,0:T(8,128)(2,1)S(1)} custom-call(s32[2]{0:T(128)S(1)} %pad_add_fusion.place.refs_0_, f32[2,64,32]{2,1,0:T(8,128)S(1)} %copy-done.8, f32[2,64,64]{2,1,0:T(8,128)S(1)} %copy-done.5, bf16[32,32,128]{2,1,0:T(8,128)(2,1)S(1)} %get-tuple-element.21.refs_3_, bf16[32,32,128]{2,1,0:T(8,128)(2,1)S(1)} %collective-permute-done.2.refs_4_, ...), custom_call_target="tpu_custom_call" | custom-call | tf_op jit(solution)/shard_map/x_forward/pallas_call | solution.py:156
  67.9 17.9 %all_to_all.22.sent_ref = bf16[64,40,128]{2,1,0:T(8,128)(2,1)S(1)} all-to-all(bf16[64,40,128]{2,1,0:T(8,128)(2,1)S(1)} %x_forward.3), channel_id=1, replica_groups=mesh['gx'=64,'gy'=2] {'gx'}, dimensions={0} | all-to-all | bytes 1310720 | tf_op jit(solution)/shard_map/all_to_all | solution.py:498
  85.8 1.0 mix_back.1
  86.8 17.0 %all_to_all.23.sent_ref = bf16[64,40,128]{2,1,0:T(8,128)(2,1)S(1)} all-to-all(bf16[64,40,128]{2,1,0:T(8,128)(2,1)S(1)} %get-tuple-element.24), channel_id=1, replica_groups=mesh['gx'=64,'gy'=2] {'gx'}, dimensions={0} | all-to-all | bytes 1310720 | tf_op jit(solution)/shard_map/all_to_all | solution.py:498
  103.8 1.4 %x_inverse.3.own_in_ref = bf16[34,32,128]{2,1,0:T(8,128)(2,1)S(1)} custom-call(s32[2]{0:T(128)S(1)} %pad_add_fusion.place.refs_0_, f32[2,32,64]{2,1,0:T(8,128)S(1)} %copy-done.9, f32[2,64,64]{2,1,0:T(8,128)S(1)} %copy-done.5, bf16[64,40,128]{2,1,0:T(8,128)(2,1)S(1)} %all_to_all.23.sent_ref), custom_call_target="tpu_custom_call" | custom-call | tf_op jit(solution)/shard_map/x_inverse/pallas_call | solution.py:190
  105.1 3.2 %collective-permute-start.3 = (bf16[34,32,128]{2,1,0:T(8,128)(2,1)S(1)}, bf16[34,32,128]{2,1,0:T(8,128)(2,1)S(1)}, u32[]{:S(2)}, u32[]{:S(2)}) collective-permute-start(bf16[34,32,128]{2,1,0:T(8,128)(2,1)S(1)} %x_inverse.3.own_in_ref), channel_id=1, source_target_pairs={{0,1},{1,0},{2,3},{3,2},{4,5},{5,4},{6,7},{7,6},{8,9},{9,8},{10,11... | collective-permute-start | bytes 835592 | tf_op jit(solution)/shard_map/ppermute | solution.py:494
  108.4 2.1 %outer.1 = f32[32,64,128]{2,1,0:T(8,128)} custom-call(bf16[64,64]{1,0:T(8,128)(2,1)S(1)} %get-tuple-element.26.spectrum_ref, bf16[64,128]{1,0:T(8,128)(2,1)S(1)} %get-tuple-element.27.pair_ref), custom_call_target="tpu_custom_call" | custom-call | flops 33554432 | bytes 1048576 | tf_op jit(solution)/shard_map/outer/pallas_call | solution.py:291
  110.5 4.9 %last_step.1 = (bf16[64,32,1024]{2,1,0:T(8,128)(2,1)}, f32[64,64]{1,0:T(8,128)}) custom-call(s32[2]{0:T(128)S(1)} %pad_add_fusion.place.refs_0_, bf16[32,64,1024]{2,1,0:T(8,128)(2,1)S(1)} %get-tuple-element.20.slope_ref, bf16[34,32,128]{2,1,0:T(8,128)(2,1)S(1)} %x_inverse.3.own_in_ref, bf16[34,32,128]{2,1,0:T(8,128)(2,1)S(1)} %collective-permute-done.3.other_in_ref, ...), custom_call_target="tpu_custom_call" | custom-call | tf_op jit(solution)/shard_map/last_step/pallas_call | solution.py:475
  (21 shorter events, 0.1 us)
Async XLA Ops:
  0.6 34.2 %copy-start.1 = (bf16[1,32,64,128]{3,2,1,0:T(8,128)(2,1)S(1)}, bf16[1,32,64,128]{3,2,1,0:T(8,128)(2,1)}, u32[]{:S(2)}) copy-start(bf16[1,32,64,128]{3,2,1,0:T(8,128)(2,1)} %param.12) | copy-start | bytes 1572868
  0.7 1.0 copy-start.2
  1.7 55.4 %copy-start = (bf16[1,64,32,1024]{3,2,1,0:T(8,128)(2,1)S(1)}, bf16[1,64,32,1024]{3,2,1,0:T(8,128)(2,1)}, u32[]{:S(2)}) copy-start(bf16[1,64,32,1024]{3,2,1,0:T(8,128)(2,1)} %param.10) | copy-start | bytes 12582916
  1.7 55.4 %copy-start.3 = (bf16[1024,128]{1,0:T(8,128)(2,1)S(1)}, bf16[1024,128]{1,0:T(8,128)(2,1)}, u32[]{:S(2)}) copy-start(bf16[1024,128]{1,0:T(8,128)(2,1)} %constant.18.clone.forth_ref) | copy-start | bytes 786436
  6.0 2.7 %collective-permute-start = (bf16[32,32,128]{2,1,0:T(8,128)(2,1)S(1)}, bf16[32,32,128]{2,1,0:T(8,128)(2,1)S(1)}, u32[]{:S(2)}, u32[]{:S(2)}) collective-permute-start(bf16[32,32,128]{2,1,0:T(8,128)(2,1)S(1)} %get-tuple-element.18), channel_id=1, source_target_pairs={{0,1},{1,0},{2,3},{3,2},{4,5},{5,4},{6,7},{7,6},{8,9},{9,8},{10,11... | collective-permute-start | bytes 786440 | tf_op jit(solution)/shard_map/ppermute | solution.py:494
  8.7 0.8 copy-start.4
  9.5 0.8 copy-start.7
  10.4 40.9 %copy-start.5 = (f32[2,64,64]{2,1,0:T(8,128)S(1)}, f32[2,64,64]{2,1,0:T(8,128)}, u32[]{:S(2)}) copy-start(f32[2,64,64]{2,1,0:T(8,128)} %constant.22.clone.refs_2_.origin_ref) | copy-start | bytes 98308
  10.4 40.9 %copy-start.9 = (f32[2,32,64]{2,1,0:T(8,128)S(1)}, f32[2,32,64]{2,1,0:T(8,128)}, u32[]{:S(2)}) copy-start(f32[2,32,64]{2,1,0:T(8,128)} %constant.20.clone.phase_ref) | copy-start | bytes 49156
  10.4 46.8 %copy-start.6 = (bf16[128,1024]{1,0:T(8,128)(2,1)S(1)}, bf16[128,1024]{1,0:T(8,128)(2,1)}, u32[]{:S(2)}) copy-start(bf16[128,1024]{1,0:T(8,128)(2,1)} %constant.19.clone.back_ref) | copy-start | bytes 786436
  10.4 46.8 %copy-start.10 = (bf16[64,64]{1,0:T(8,128)(2,1)S(1)}, bf16[64,64]{1,0:T(8,128)(2,1)}, u32[]{:S(2)}) copy-start(bf16[64,64]{1,0:T(8,128)(2,1)} %local_ref.3) | copy-start | bytes 24580
  52.6 4.5 %collective-permute-start.1 = (bf16[32,32,128]{2,1,0:T(8,128)(2,1)S(1)}, bf16[32,32,128]{2,1,0:T(8,128)(2,1)S(1)}, u32[]{:S(2)}, u32[]{:S(2)}) collective-permute-start(bf16[32,32,128]{2,1,0:T(8,128)(2,1)S(1)} %x_inverse.2.own_in_ref), channel_id=1, source_target_pairs={{0,1},{1,0},{2,3},{3,2},{4,5},{5,4},{6,7},{7,6},{8,9},{9,8},{10,11... | collective-permute-start | bytes 786440 | tf_op jit(solution)/shard_map/ppermute | solution.py:494
  57.2 9.5 %copy-start.8 = (f32[2,64,32]{2,1,0:T(8,128)S(1)}, f32[2,64,32]{2,1,0:T(8,128)}, u32[]{:S(2)}) copy-start(f32[2,64,32]{2,1,0:T(8,128)} %constant.21.clone.refs_1_) | copy-start | bytes 49156
  64.9 1.8 %collective-permute-start.2 = (bf16[32,32,128]{2,1,0:T(8,128)(2,1)S(1)}, bf16[32,32,128]{2,1,0:T(8,128)(2,1)S(1)}, u32[]{:S(2)}, u32[]{:S(2)}) collective-permute-start(bf16[32,32,128]{2,1,0:T(8,128)(2,1)S(1)} %get-tuple-element.22), channel_id=1, source_target_pairs={{0,1},{1,0},{2,3},{3,2},{4,5},{5,4},{6,7},{7,6},{8,9},{9,8},{10,11... | collective-permute-start | bytes 786440 | tf_op jit(solution)/shard_map/ppermute | solution.py:494
  105.1 5.4 %collective-permute-start.3 = (bf16[34,32,128]{2,1,0:T(8,128)(2,1)S(1)}, bf16[34,32,128]{2,1,0:T(8,128)(2,1)S(1)}, u32[]{:S(2)}, u32[]{:S(2)}) collective-permute-start(bf16[34,32,128]{2,1,0:T(8,128)(2,1)S(1)} %x_inverse.3.own_in_ref), channel_id=1, source_target_pairs={{0,1},{1,0},{2,3},{3,2},{4,5},{5,4},{6,7},{7,6},{8,9},{9,8},{10,11... | collective-permute-start | bytes 835592 | tf_op jit(solution)/shard_map/ppermute | solution.py:494

commit v2 on v1

--- a/solution.py
+++ b/solution.py
@@ -38,7 +38,11 @@
     xangle = (frequency[:, None] * np.arange(XC)[None, :] % NX) * (TWO_PI / NX)
     phase = np.stack([np.cos(xangle), np.sin(xangle)])
     origin = (modes[:, None] * np.arange(SHARDS)[None, :] % SHARDS) * (TWO_PI / SHARDS)
-    return forth, forth.T, phase, np.stack([np.cos(origin), np.sin(origin)])
+    packed = np.zeros((2, 160, 128))
+    packed[:, :64, :XC] = phase
+    packed[:, 64:96, :MX] = np.transpose(phase, (0, 2, 1))
+    packed[:, 96:, :SHARDS] = np.stack([np.cos(origin), np.sin(origin)])
+    return forth, forth.T, packed
 
 
 def dot(a, b, dims=((1,), (0,))):
@@ -78,15 +82,61 @@
     return own.reshape(shape).astype(BF), other.reshape(shape).astype(BF)
 
 
-def y_forward_kernel(place, field_ref, forth_ref, cells_ref, own_ref, other_ref, held, arrived):
+def rotated(phase_ref, shard, rows, columns, axis):
+    at = iota((MX, SHARDS), 1 - axis) == shard
+    cosine, sine = [
+        jnp.sum(jnp.where(at, phase_ref[q, 96:, :SHARDS], 0.0), axis=1 - axis, keepdims=True) for q in range(2)
+    ]
+    real, imag = [phase_ref[q, rows, :columns] for q in range(2)]
+    return (cosine * real - sine * imag).astype(BF), (sine * real + cosine * imag).astype(BF)
+
+
+def x_matrices(phase_ref, shard):
+    widen = (iota((XC, 256), 1) // 8 == iota((XC, 256), 0)).astype(BF)
+    keep = iota((1, 8, 256), 2) % 8 == iota((1, 8, 256), 1)
+    forward = []
+    for table in rotated(phase_ref, shard, slice(0, 64), XC, 0):
+        wide = dot(table, widen)
+        forward.append(jnp.where(keep, wide[:, None, :], 0.0).reshape(512, 256).astype(BF))
+    widen = (iota((MX, 512), 1) // 8 == iota((MX, 512), 0)).astype(BF)
+    keep = iota((1, 8, 512), 2) % 8 == iota((1, 8, 512), 1)
+    inverse = []
+    for table in rotated(phase_ref, shard, slice(64, 96), MX, 1):
+        wide = dot(table, widen)
+        inverse.append(jnp.where(keep, wide[:, None, :], 0.0).reshape(256, 512).astype(BF))
+    return jnp.concatenate(forward, axis=1), jnp.concatenate(inverse, axis=0)
+
+
+def y_forward_kernel(
+    place,
+    field_ref,
+    table_ref,
+    phase_ref,
+    cells_ref,
+    own_ref,
+    other_ref,
+    forth_ref,
+    forward_ref,
+    inverse_ref,
+    held,
+    phase,
+    arrived,
+):
     def copy(k):
         group, half = k // 2, k % 2
         channels = pl.ds(pl.multiple_of(32 * group, 32), 32)
         cells = pl.ds(pl.multiple_of(16 * half, 16), 16)
         return pltpu.make_async_copy(field_ref.at[channels, cells], held.at[k], arrived.at[k])
 
+    copy_phase = pltpu.make_async_copy(phase_ref, phase, arrived.at[4])
+    copy_table = pltpu.make_async_copy(table_ref, forth_ref, arrived.at[5])
+    copy_phase.start()
+    copy_table.start()
     for k in range(4):
         copy(k).start()
+    copy_phase.wait()
+    forward_ref[...], inverse_ref[...] = x_matrices(phase, place[0])
+    copy_table.wait()
 
     @pl.loop(0, 4)
     def _(k):
@@ -102,41 +152,35 @@
         other_ref[cells, channels, :] = other
 
 
-def y_forward(place, field, forth):
+def y_forward(place, field, forth, phase):
+    away = pl.BlockSpec(memory_space=pltpu.HBM)
+    operands = [pltpu.with_memory_space_constraint(a, pltpu.HBM) for a in (field, forth, phase)]
     return pl.pallas_call(
         y_forward_kernel,
-        in_specs=[SMEM, pl.BlockSpec(memory_space=pltpu.HBM), VMEM],
-        out_specs=[VMEM, VMEM, VMEM],
+        in_specs=[SMEM, away, away, away],
+        out_specs=[VMEM] * 6,
         out_shape=[
             pltpu.VMEM((XC, C, YC), BF),
             pltpu.VMEM((XC, 32, 128), BF),
             pltpu.VMEM((XC, 32, 128), BF),
+            pltpu.VMEM((YC, 128), BF),
+            pltpu.VMEM((512, 512), BF),
+            pltpu.VMEM((512, 512), BF),
         ],
-        scratch_shapes=[pltpu.VMEM((4, 32, 16, YC), BF), pltpu.SemaphoreType.DMA((4,))],
+        scratch_shapes=[
+            pltpu.VMEM((4, 32, 16, YC), BF),
+            pltpu.VMEM((2, 160, 128), F32),
+            pltpu.SemaphoreType.DMA((6,)),
+        ],
         compiler_params=pltpu.CompilerParams(vmem_limit_bytes=16 << 20),
         name="y_forward",
-    )(place, pltpu.with_memory_space_constraint(field, pltpu.HBM), forth)
-
-
-def rotated(phase_ref, origin_ref, shard, axis):
-    at = iota((MX, SHARDS), 1 - axis) == shard
-    cosine, sine = [
-        jnp.sum(jnp.where(at, origin_ref[q], 0.0), axis=1 - axis, keepdims=True) for q in range(2)
-    ]
-    real, imag = phase_ref[0], phase_ref[1]
-    return (cosine * real - sine * imag).astype(BF), (sine * real + cosine * imag).astype(BF)
-
-
-def x_forward_kernel(scale, place, phase_ref, origin_ref, own_ref, other_ref, *rest):
+    )(place, *operands)
+
+
+def x_forward_kernel(scale, left_ref, own_ref, other_ref, *rest):
     out_ref = rest[-1]
     total = own_ref[...].astype(F32) + other_ref[...].astype(F32)
-    widen = (iota((XC, 256), 1) // 8 == iota((XC, 256), 0)).astype(BF)
-    keep = iota((1, 8, 256), 2) % 8 == iota((1, 8, 256), 1)
-    left = []
-    for table in rotated(phase_ref, origin_ref, place[0], 0):
-        wide = dot(table, widen)
-        left.append(jnp.where(keep, wide[:, None, :], 0.0).reshape(512, 256).astype(BF))
-    left = jnp.concatenate(left, axis=1)
+    left = left_ref[...]
     for g in range(2):
         right = []
         for s in range(2):
@@ -150,27 +194,21 @@
         out_ref[:, 32:, :] = jnp.broadcast_to(rider[:, None, :], (64, RIDER, 128)).astype(BF)
 
 
-def x_forward(place, phase, origin, own, other, scale, rider=None):
+def x_forward(left, own, other, scale, rider=None):
     rows = 32 if rider is None else 32 + RIDER
     operands = [own, other] + ([] if rider is None else [rider])
     return pl.pallas_call(
         lambda *refs: x_forward_kernel(scale, *refs),
-        in_specs=[SMEM, VMEM, VMEM] + [VMEM] * len(operands),
+        in_specs=[VMEM] * (1 + len(operands)),
         out_specs=VMEM,
         out_shape=pltpu.VMEM((SHARDS, rows, 128), BF),
         compiler_params=pltpu.CompilerParams(vmem_limit_bytes=16 << 20),
         name="x_forward",
-    )(place, phase, origin, *operands)
-
-
-def x_inverse_kernel(place, phase_ref, origin_ref, sent_ref, inner_ref):
-    widen = (iota((MX, 512), 1) // 8 == iota((MX, 512), 0)).astype(BF)
-    keep = iota((1, 8, 512), 2) % 8 == iota((1, 8, 512), 1)
-    left = []
-    for table in rotated(phase_ref, origin_ref, place[0], 1):
-        wide = dot(table, widen)
-        left.append(jnp.where(keep, wide[:, None, :], 0.0).reshape(256, 512).astype(BF))
-    left = jnp.concatenate(left, axis=0)
+    )(left, *operands)
+
+
+def x_inverse_kernel(left_ref, sent_ref, inner_ref):
+    left = left_ref[...]
     for g in range(2):
         rows = sent_ref[:, 16 * g : 16 * g + 16, :].astype(F32)
         right = [rows[:, 8 * s : 8 * s + 8].reshape(512, 128) for s in range(2)]
@@ -185,16 +223,16 @@
         inner_ref[XC:, :, :] = rider.reshape(2, 32, 128).astype(BF)
 
 
-def x_inverse(place, phase, origin, sent):
+def x_inverse(left, sent):
     cells = XC if sent.shape[1] == 32 else XC + 2
     return pl.pallas_call(
         x_inverse_kernel,
-        in_specs=[SMEM, VMEM, VMEM, VMEM],
+        in_specs=[VMEM, VMEM],
         out_specs=VMEM,
         out_shape=pltpu.VMEM((cells, 32, 128), BF),
         compiler_params=pltpu.CompilerParams(vmem_limit_bytes=16 << 20),
         name="x_inverse",
-    )(place, phase, origin, sent)
+    )(left, sent)
 
 
 def pick(b):
@@ -278,26 +316,75 @@
     )(sent, weights)
 
 
-def outer_kernel(spectrum_ref, pair_ref, out_ref):
+def outer_kernel(spectrum_ref, pair_ref, out_ref, staged, sent):
     flipped = spectrum_ref[...].astype(F32).T
-    tall = jnp.concatenate([flipped] * 8, axis=0)
-    shape = tall.shape
-    keep = iota(shape, 1) % 32 == iota(shape, 0) // C + 8 * pl.program_id(0)
-    tall = jnp.where(keep, tall, 0.0).astype(BF)
-    out_ref[...] = (dot(tall, pair_ref[...]) * GAMMA).reshape(8, C, 128)
+    tall = jnp.concatenate([flipped] * 16, axis=0)
+
+    def copy(k):
+        piece = slice(16 * k, 16 * k + 16)
+        return pltpu.make_async_copy(staged.at[piece], out_ref.at[piece], sent.at[k])
+
+    for k in range(2):
+        keep = iota(tall.shape, 1) % 32 == iota(tall.shape, 0) // C + 16 * k
+        rows = jnp.where(keep, tall, 0.0).astype(BF)
+        staged[16 * k : 16 * k + 16] = (dot(rows, pair_ref[...]) * GAMMA).reshape(16, C, 128)
+        copy(k).start()
+    for k in range(2):
+        copy(k).wait()
 
 
 def outer(spectrum, pair):
     return pl.pallas_call(
         outer_kernel,
-        grid=(4,),
-        in_specs=[pl.BlockSpec((64, C), lambda i: (0, 0)), pl.BlockSpec((64, 128), lambda i: (0, 0))],
-        out_specs=pl.BlockSpec((8, C, 128), lambda i: (i, 0, 0)),
+        in_specs=[VMEM, VMEM],
+        out_specs=pl.BlockSpec(memory_space=pltpu.HBM),
         out_shape=jax.ShapeDtypeStruct((32, C, 128), F32),
-        compiler_params=pltpu.CompilerParams(vmem_limit_bytes=20 << 20),
-        cost_estimate=pl.CostEstimate(flops=2 * 2048 * 64 * 128, bytes_accessed=1 << 20, transcendentals=0),
+        scratch_shapes=[pltpu.VMEM((32, C, 128), F32), pltpu.SemaphoreType.DMA((2,))],
+        compiler_params=pltpu.CompilerParams(vmem_limit_bytes=16 << 20),
+        cost_estimate=pl.CostEstimate(flops=1 << 30, bytes_accessed=1 << 20, transcendentals=0),
         name="outer",
     )(spectrum, pair)
+
+
+def relaid_kernel(cells_ref, after_ref, out_ref):
+    out_ref[...] = jnp.swapaxes(cells_ref[...], 0, 1)
+
+
+def relaid(cells, after):
+    return pl.pallas_call(
+        relaid_kernel,
+        in_specs=[VMEM, pl.BlockSpec(memory_space=pl.ANY)],
+        out_specs=VMEM,
+        out_shape=pltpu.VMEM((XC, C, YC), BF),
+        compiler_params=pltpu.CompilerParams(vmem_limit_bytes=16 << 20),
+        cost_estimate=pl.CostEstimate(flops=1 << 30, bytes_accessed=8 << 20, transcendentals=0),
+        name="relaid",
+    )(cells, after)
+
+
+def weight_kernel(field_ref, slope_ref, weight_ref):
+    products = jnp.zeros((256, 256), F32)
+    for g in range(XC // 4):
+        field = field_ref[4 * g : 4 * g + 4].reshape(256, YC)
+        slope = slope_ref[4 * g : 4 * g + 4].reshape(256, YC)
+        products = products + dot(field, slope, ((1,), (1,)))
+    total = products[:64, :128] + pltpu.roll(products[64:128, :128], 64, 1)
+    total = total + products[128:192, 128:] + pltpu.roll(products[192:, 128:], 64, 1)
+    high = total.astype(BF).astype(F32)
+    low = pltpu.roll(total - high, 64, 1)
+    weight_ref[...] = jnp.where(iota((64, 128), 1) < 64, high, low).astype(BF)
+
+
+def weight_step(cells, slope):
+    return pl.pallas_call(
+        weight_kernel,
+        in_specs=[VMEM, VMEM],
+        out_specs=VMEM,
+        out_shape=pltpu.VMEM((64, 128), BF),
+        compiler_params=pltpu.CompilerParams(vmem_limit_bytes=16 << 20),
+        cost_estimate=pl.CostEstimate(flops=1 << 30, bytes_accessed=8 << 20, transcendentals=0),
+        name="weight_step",
+    )(cells, slope)
 
 
 def gelu_slope(values):
@@ -347,14 +434,12 @@
     slope_ref,
     own_ref,
     other_ref,
-    weight_ref,
     inner,
 ):
     diagonal = block_diagonal(local_ref[...].astype(F32)).T.astype(BF)
     inner_rows(place[1], INVERSE, own_in_ref, other_in_ref, inner)
-    products = jnp.zeros((256, 256), F32)
     tiles = [(half, y, g) for half in range(2) for y in range(YC // YB) for g in range(4)]
-    flipped, ready, made = {}, {}, {}
+    ready, made = {}, {}
     sums = {}
 
     def place_of(tile):
@@ -365,56 +450,46 @@
     def begin(tile):
         half, y, g = tile
         cells, rows, columns = place_of(tile)
-        if g == 0:
-            flipped[half, y] = jnp.swapaxes(cotangent_ref[:, 16 * half : 16 * half + 16, columns], 0, 1)
         field = field_ref[cells, :, columns].reshape(256, YB)
         ready[tile] = mixed_cells(diagonal, inner, field, back_ref[:, columns], rows.start)
 
     def bend(tile):
         half, y, g = tile
         cells, rows, columns = place_of(tile)
-        upper = flipped[half, y][4 * g : 4 * g + 4].reshape(256, YB).astype(F32)
+        upper = cotangent_ref[cells, :, columns].reshape(256, YB).astype(F32)
         slope = (upper * gelu_slope(ready.pop(tile))).astype(BF)
         slope_ref[cells, :, columns] = slope.reshape(4, C, YB)
         made[tile] = slope
 
-    def end(tile, products):
+    def end(tile):
         half, y, g = tile
         cells, rows, columns = place_of(tile)
         slope = made.pop(tile)
-        field = field_ref[cells, :, columns].reshape(256, YB)
         part = dot(slope, forth_ref[columns, :])
         sums[half, g] = part if y == 0 else sums[half, g] + part
-        return products + dot(field, slope, ((1,), (1,)))
 
     for t in range(len(tiles) + 2):
         if t < len(tiles):
             begin(tiles[t])
         if t >= 2:
-            products = end(tiles[t - 2], products)
+            end(tiles[t - 2])
         if 1 <= t <= len(tiles):
             bend(tiles[t - 1])
     for half in range(2):
         cells = slice(16 * half, 16 * half + 16)
         parts = jnp.concatenate([sums[half, g] for g in range(4)], axis=0)
         own_ref[cells], other_ref[cells] = split_halves(parts, 16, 4, place[1])
-    total = products[:64, :128] + pltpu.roll(products[64:128, :128], 64, 1)
-    total = total + products[128:192, 128:] + pltpu.roll(products[192:, 128:], 64, 1)
-    high = total.astype(BF).astype(F32)
-    low = pltpu.roll(total - high, 64, 1)
-    weight_ref[...] = jnp.where(iota((64, 128), 1) < 64, high, low).astype(BF)
 
 
 def cells_step(place, cells, cotangent, own, other, local_weight, forth, back):
     return pl.pallas_call(
         cells_kernel,
         in_specs=[SMEM] + [VMEM] * 7,
-        out_specs=[VMEM] * 4,
+        out_specs=[VMEM] * 3,
         out_shape=[
             pltpu.VMEM((XC, C, YC), BF),
             pltpu.VMEM((XC, 32, 128), BF),
             pltpu.VMEM((XC, 32, 128), BF),
-            pltpu.VMEM((64, 128), BF),
         ],
         scratch_shapes=[pltpu.VMEM((XC * C, 128), BF)],
         compiler_params=pltpu.CompilerParams(vmem_limit_bytes=24 << 20),
@@ -499,25 +574,27 @@
 
 
 def on_device(field, cotangent, local_weight, spectral_weight):
-    forth, back, phase, origin = tables()
+    forth, back, phase = tables()
     forth, back = [jnp.asarray(t.astype(np.float32), BF) for t in (forth, back)]
-    phase_back = jnp.asarray(np.transpose(phase, (0, 2, 1)), F32)
-    phase, origin = [jnp.asarray(t, F32) for t in (phase, origin)]
+    phase = jnp.asarray(phase, F32)
     place = jnp.stack([lax.axis_index("gx"), lax.axis_index("gy")]).astype(jnp.int32)
     weights = spectral_weight[0]
 
-    cells, own, other = y_forward(place, field[0], forth)
-    sent = exchange(x_forward(place, phase, origin, own, swap_cores(other), FORWARD))
+    cells, own, other, forth, forward, inverse = y_forward(place, field[0], forth, phase)
+    sent = exchange(x_forward(forward, own, swap_cores(other), FORWARD))
     copies, spectrum = mix(sent, weights)
-    inner = x_inverse(place, phase_back, origin, exchange(copies))
-    slope, own, other, rider = cells_step(
-        place, cells, cotangent[0], inner, swap_cores(inner), local_weight, forth, back
-    )
-    sent = exchange(x_forward(place, phase, origin, own, swap_cores(other), INVERSE, rider))
+    inner = x_inverse(inverse, exchange(copies))
+    other = swap_cores(inner)
+    upper = relaid(cotangent[0], inner)
+    slope, own, other = cells_step(place, cells, upper, inner, other, local_weight, forth, back)
+    other = swap_cores(other)
+    rider = weight_step(cells, slope)
+    sent = exchange(x_forward(forward, own, other, INVERSE, rider))
     copies, pair = mix_back(sent, weights)
-    inner = x_inverse(place, phase_back, origin, exchange(copies))
+    inner = x_inverse(inverse, exchange(copies))
+    other = swap_cores(inner)
     grad_spectral = outer(spectrum, pair)
-    grad_field, grad_local = last_step(place, slope, inner, swap_cores(inner), local_weight, back)
+    grad_field, grad_local = last_step(place, slope, inner, other, local_weight, back)
     return (grad_field[None], grad_spectral[None], grad_local)
 
 

time: 116 us -> 109 us (0.940)
  local copies, waits for them, and re-layouts: 2.71 us -> 0.02 us
  waiting for transfers between devices: 3.49 us -> 1.17 us
  Pallas kernels: 26.1 us -> 24.1 us
    unnamed x22 -> x8, local copies, waits for them, and re-layouts: 2.71 us -> 0.02 us
    ppermute x4, waiting for transfers between devices: 3.49 us -> 1.17 us  [swap_cores(): return lax.ppermute(values, 'gy', [(0, 1), (1, 0)])]
    pallas_call x1, Pallas kernels: 7.7 us -> 6.2 us  [cells_step(): pl.pallas_call(cells_kernel, in_specs=[SMEM] + [VMEM] * 7, out_specs=[VME...]
    pallas_call x6 -> x8, Pallas kernels: 11.5 us -> 11 us  [the longest x1 4.5 us: y_forward(): pl.pallas_call(y_forward_kernel, in_specs=[SMEM, away, away, away], out_s...]
  transfers between devices with their start and end apart: 4 -> 4, of which waited for: 3 -> 1; matrix products, arithmetic and copies ran while one was open for 0% -> 0% of each run, Pallas kernels for 2% -> 4%
where the time goes in v2:
time: 109 us
  blocking collectives  73.8 us (68%)
  Pallas kernels  24.1 us (22%)
  starting transfers between devices  8.72 us (8%)
  waiting for transfers between devices  1.17 us (1%)
    all_to_all x4, blocking collectives, exchange(): return lax.all_to_all(rows, 'gx', 0, 0, tiled=True)  73.8 us
    ppermute x4, starting transfers between devices, swap_cores(): return lax.ppermute(values, 'gy', [(0, 1), (1, 0)])  8.72 us
    pallas_call x1, Pallas kernels, cells_step(): pl.pallas_call(cells_kernel, in_specs=[SMEM] + [VMEM] * 7, out_specs=[VME...  6.2 us
    pallas_call x1, Pallas kernels, last_step(): pl.pallas_call(last_kernel, in_specs=[SMEM] + [VMEM] * 5, out_specs=[pl.B...  4.93 us
    pallas_call x1, Pallas kernels, y_forward(): pl.pallas_call(y_forward_kernel, in_specs=[SMEM, away, away, away], out_s...  4.5 us
  transfers between devices with their start and end apart: 4, of which 1 were waited for; matrix products, arithmetic and copies ran while one was open for 0% of the time, Pallas kernels for 4%

profile of v2, /device:TPU:1, one launch (start us, length us, event | category | flops | bytes accessed | tf_op | source)
XLA Modules:
  0.0 108.8 jit_solution(17256083269369230095)
XLA Ops:
  0.6 0.1 pad_add_fusion.place
  0.7 4.5 %y_forward.1 = (bf16[32,64,1024]{2,1,0:T(8,128)(2,1)S(1)}, bf16[32,32,128]{2,1,0:T(8,128)(2,1)S(1)}, bf16[32,32,128]{2,1,0:T(8,128)(2,1)S(1)}, bf16[1024,128]{1,...) custom-call(s32[2]{0:T(128)S(1)} %pad_add_fusion.place, bf16[64,32,1024]{2,1,0:T(8,128)(2,1)} %bitcast.10, ...), custom_call_target="tpu_custom_call" | custom-call | tf_op jit(solution)/shard_map/y_forward/pallas_call | solution.py:158
  5.2 1.5 %collective-permute-start = (bf16[32,32,128]{2,1,0:T(8,128)(2,1)S(1)}, bf16[32,32,128]{2,1,0:T(8,128)(2,1)S(1)}, u32[]{:S(2)}, u32[]{:S(2)}) collective-permute-start(bf16[32,32,128]{2,1,0:T(8,128)(2,1)S(1)} %get-tuple-element.22), channel_id=1, source_target_pairs={{0,1},{1,0},{2,3},{3,2},{4,5},{5,4},{6,7},{7,6},{8,9},{9,8},{10,11... | collective-permute-start | bytes 786440 | tf_op jit(solution)/shard_map/ppermute | solution.py:569
  6.7 1.2 %collective-permute-done.refs_2_ = bf16[32,32,128]{2,1,0:T(8,128)(2,1)S(1)} collective-permute-done((bf16[32,32,128]{2,1,0:T(8,128)(2,1)S(1)}, bf16[32,32,128]{2,1,0:T(8,128)(2,1)S(1)}, u32[]{:S(2)}, u32[]{:S(2)}) %collective-permute-start) | collective-permute-done | bytes 262176 | tf_op jit(solution)/shard_map/ppermute | solution.py:569
  7.9 0.6 x_forward.2
  8.5 23.3 %all_to_all.20.sent_ref = bf16[64,32,128]{2,1,0:T(8,128)(2,1)S(1)} all-to-all(bf16[64,32,128]{2,1,0:T(8,128)(2,1)S(1)} %x_forward.2), channel_id=1, replica_groups=mesh['gx'=64,'gy'=2] {'gx'}, dimensions={0} | all-to-all | bytes 1048576 | tf_op jit(solution)/shard_map/all_to_all | solution.py:573
  31.7 1.0 mix.1
  32.7 15.4 %all_to_all.21.sent_ref = bf16[64,32,128]{2,1,0:T(8,128)(2,1)S(1)} all-to-all(bf16[64,32,128]{2,1,0:T(8,128)(2,1)S(1)} %get-tuple-element.23), channel_id=1, replica_groups=mesh['gx'=64,'gy'=2] {'gx'}, dimensions={0} | all-to-all | bytes 1048576 | tf_op jit(solution)/shard_map/all_to_all | solution.py:573
  48.1 0.7 x_inverse.2.after_ref.own_in_ref
  48.8 3.4 %collective-permute-start.1 = (bf16[32,32,128]{2,1,0:T(8,128)(2,1)S(1)}, bf16[32,32,128]{2,1,0:T(8,128)(2,1)S(1)}, u32[]{:S(2)}, u32[]{:S(2)}) collective-permute-start(bf16[32,32,128]{2,1,0:T(8,128)(2,1)S(1)} %x_inverse.2.after_ref.own_in_ref), channel_id=1, source_target_pairs={{0,1},{1,0},{2,3},{3,2},{4,5},{5,4},{6,7},{7,6},{8,9},{9,8},{10,11... | collective-permute-start | bytes 786440 | tf_op jit(solution)/shard_map/ppermute | solution.py:569
  52.2 1.2 %relaid.1.cotangent_ref = bf16[32,64,1024]{2,1,0:T(8,128)(2,1)S(1)} custom-call(bf16[64,32,1024]{2,1,0:T(8,128)(2,1)S(1)} %bitcast.7, bf16[32,32,128]{2,1,0:T(8,128)(2,1)S(1)} %x_inverse.2.after_ref.own_in_ref), custom_call_target="tpu_custom_call" | custom-call | flops 1073741824 | bytes 8388608 | tf_op jit(solution)/shard_map/relaid/pallas_call | solution.py:354
  53.4 0.0 collective-permute-done.1.other_in_ref
  53.4 6.2 %cells_step.1 = (bf16[32,64,1024]{2,1,0:T(8,128)(2,1)S(1)}, bf16[32,32,128]{2,1,0:T(8,128)(2,1)S(1)}, bf16[32,32,128]{2,1,0:T(8,128)(2,1)S(1)}) custom-call(s32[2]{0:T(128)S(1)} %pad_add_fusion.place, bf16[32,64,1024]{2,1,0:T(8,128)(2,1)S(1)} %get-tuple-element.18.field_ref, bf16[32,64,1024]{2,1,0:T(8,128)(2,1)S(1)} %relaid.1.cotangent_ref, ...), custom_call_target="tpu_custom_call" | custom-call | tf_op jit(solution)/shard_map/cells_step/pallas_call | solution.py:485
  59.6 0.6 collective-permute-start.2
  60.2 1.4 %weight_step.1.refs_3_ = bf16[64,128]{1,0:T(8,128)(2,1)S(1)} custom-call(bf16[32,64,1024]{2,1,0:T(8,128)(2,1)S(1)} %get-tuple-element.18.field_ref, bf16[32,64,1024]{2,1,0:T(8,128)(2,1)S(1)} %get-tuple-element.25.slope_ref), custom_call_target="tpu_custom_call" | custom-call | flops 1073741824 | bytes 8388608 | tf_op jit(solution)/shard_map/weight_step/pallas_call | solution.py:379
  61.7 0.6 x_forward.3
  62.2 18.1 %all_to_all.22.sent_ref = bf16[64,40,128]{2,1,0:T(8,128)(2,1)S(1)} all-to-all(bf16[64,40,128]{2,1,0:T(8,128)(2,1)S(1)} %x_forward.3), channel_id=1, replica_groups=mesh['gx'=64,'gy'=2] {'gx'}, dimensions={0} | all-to-all | bytes 1310720 | tf_op jit(solution)/shard_map/all_to_all | solution.py:573
  80.4 1.0 mix_back.1
  81.4 17.0 %all_to_all.23.sent_ref = bf16[64,40,128]{2,1,0:T(8,128)(2,1)S(1)} all-to-all(bf16[64,40,128]{2,1,0:T(8,128)(2,1)S(1)} %get-tuple-element.28), channel_id=1, replica_groups=mesh['gx'=64,'gy'=2] {'gx'}, dimensions={0} | all-to-all | bytes 1310720 | tf_op jit(solution)/shard_map/all_to_all | solution.py:573
  98.3 0.7 x_inverse.3.own_in_ref
  99.1 3.3 %collective-permute-start.3 = (bf16[34,32,128]{2,1,0:T(8,128)(2,1)S(1)}, bf16[34,32,128]{2,1,0:T(8,128)(2,1)S(1)}, u32[]{:S(2)}, u32[]{:S(2)}) collective-permute-start(bf16[34,32,128]{2,1,0:T(8,128)(2,1)S(1)} %x_inverse.3.own_in_ref), channel_id=1, source_target_pairs={{0,1},{1,0},{2,3},{3,2},{4,5},{5,4},{6,7},{7,6},{8,9},{9,8},{10,11... | collective-permute-start | bytes 835592 | tf_op jit(solution)/shard_map/ppermute | solution.py:569
  102.3 1.3 %outer.1 = f32[32,64,128]{2,1,0:T(8,128)} custom-call(bf16[64,64]{1,0:T(8,128)(2,1)S(1)} %get-tuple-element.30.spectrum_ref, bf16[64,128]{1,0:T(8,128)(2,1)S(1)} %get-tuple-element.31.pair_ref), custom_call_target="tpu_custom_call" | custom-call | flops 1073741824 | bytes 1048576 | tf_op jit(solution)/shard_map/outer/pallas_call | solution.py:337
  103.7 0.0 collective-permute-done.3.other_in_ref
  103.7 4.9 %last_step.1 = (bf16[64,32,1024]{2,1,0:T(8,128)(2,1)}, f32[64,64]{1,0:T(8,128)}) custom-call(s32[2]{0:T(128)S(1)} %pad_add_fusion.place, bf16[32,64,1024]{2,1,0:T(8,128)(2,1)S(1)} %get-tuple-element.25.slope_ref, bf16[34,32,128]{2,1,0:T(8,128)(2,1)S(1)} %x_inverse.3.own_in_ref, bf16[34,32,128]{2,1,0:T(8,128)(2,1)S(1)} %collective-permute-done.3.other_in_ref, ...), custom_call_target="tpu_custom_call" | custom-call | tf_op jit(solution)/shard_map/last_step/pallas_call | solution.py:550
  (9 shorter events, 0.0 us)
Async XLA Ops:
  0.6 31.1 %copy-start.1 = (bf16[1,32,64,128]{3,2,1,0:T(8,128)(2,1)S(1)}, bf16[1,32,64,128]{3,2,1,0:T(8,128)(2,1)}, u32[]{:S(2)}) copy-start(bf16[1,32,64,128]{3,2,1,0:T(8,128)(2,1)} %param.10) | copy-start | bytes 1572868
  0.7 51.5 %copy-start = (bf16[1,64,32,1024]{3,2,1,0:T(8,128)(2,1)S(1)}, bf16[1,64,32,1024]{3,2,1,0:T(8,128)(2,1)}, u32[]{:S(2)}) copy-start(bf16[1,64,32,1024]{3,2,1,0:T(8,128)(2,1)} %param.8) | copy-start | bytes 12582916
  5.2 2.7 %collective-permute-start = (bf16[32,32,128]{2,1,0:T(8,128)(2,1)S(1)}, bf16[32,32,128]{2,1,0:T(8,128)(2,1)S(1)}, u32[]{:S(2)}, u32[]{:S(2)}) collective-permute-start(bf16[32,32,128]{2,1,0:T(8,128)(2,1)S(1)} %get-tuple-element.22), channel_id=1, source_target_pairs={{0,1},{1,0},{2,3},{3,2},{4,5},{5,4},{6,7},{7,6},{8,9},{9,8},{10,11... | collective-permute-start | bytes 786440 | tf_op jit(solution)/shard_map/ppermute | solution.py:569
  48.8 4.5 %collective-permute-start.1 = (bf16[32,32,128]{2,1,0:T(8,128)(2,1)S(1)}, bf16[32,32,128]{2,1,0:T(8,128)(2,1)S(1)}, u32[]{:S(2)}, u32[]{:S(2)}) collective-permute-start(bf16[32,32,128]{2,1,0:T(8,128)(2,1)S(1)} %x_inverse.2.after_ref.own_in_ref), channel_id=1, source_target_pairs={{0,1},{1,0},{2,3},{3,2},{4,5},{5,4},{6,7},{7,6},{8,9},{9,8},{10,11... | collective-permute-start | bytes 786440 | tf_op jit(solution)/shard_map/ppermute | solution.py:569
  52.2 1.2 %copy-start.2 = (bf16[128,1024]{1,0:T(8,128)(2,1)S(1)}, bf16[128,1024]{1,0:T(8,128)(2,1)}, u32[]{:S(2)}) copy-start(bf16[128,1024]{1,0:T(8,128)(2,1)} %constant.15.clone.back_ref) | copy-start | bytes 786436
  52.2 1.2 %copy-start.3 = (bf16[64,64]{1,0:T(8,128)(2,1)S(1)}, bf16[64,64]{1,0:T(8,128)(2,1)}, u32[]{:S(2)}) copy-start(bf16[64,64]{1,0:T(8,128)(2,1)} %local_ref.3) | copy-start | bytes 24580
  59.6 2.0 %collective-permute-start.2 = (bf16[32,32,128]{2,1,0:T(8,128)(2,1)S(1)}, bf16[32,32,128]{2,1,0:T(8,128)(2,1)S(1)}, u32[]{:S(2)}, u32[]{:S(2)}) collective-permute-start(bf16[32,32,128]{2,1,0:T(8,128)(2,1)S(1)} %get-tuple-element.27), channel_id=1, source_target_pairs={{0,1},{1,0},{2,3},{3,2},{4,5},{5,4},{6,7},{7,6},{8,9},{9,8},{10,11... | collective-permute-start | bytes 786440 | tf_op jit(solution)/shard_map/ppermute | solution.py:569
  99.1 4.6 %collective-permute-start.3 = (bf16[34,32,128]{2,1,0:T(8,128)(2,1)S(1)}, bf16[34,32,128]{2,1,0:T(8,128)(2,1)S(1)}, u32[]{:S(2)}, u32[]{:S(2)}) collective-permute-start(bf16[34,32,128]{2,1,0:T(8,128)(2,1)S(1)} %x_inverse.3.own_in_ref), channel_id=1, source_target_pairs={{0,1},{1,0},{2,3},{3,2},{4,5},{5,4},{6,7},{7,6},{8,9},{9,8},{10,11... | collective-permute-start | bytes 835592 | tf_op jit(solution)/shard_map/ppermute | solution.py:569

commit v3 on v2

--- a/solution.py
+++ b/solution.py
@@ -347,7 +347,7 @@
 
 
 def relaid_kernel(cells_ref, after_ref, out_ref):
-    out_ref[...] = jnp.swapaxes(cells_ref[...], 0, 1)
+    out_ref[...] = jnp.swapaxes(cells_ref[...] * jnp.asarray(0.5, BF), 0, 1)
 
 
 def relaid(cells, after):
@@ -388,10 +388,8 @@
 
 
 def gelu_slope(values):
-    return (
-        0.5 * (1.0 + lax.erf(values * ROOT_HALF))
-        + values * jnp.exp(-0.5 * values * values) * ROOT_TWO_PI
-    )
+    bell = jnp.exp2(values * values * (-0.5 / math.log(2.0)))
+    return (1.0 + lax.erf(values * ROOT_HALF)) + (values * (2.0 * ROOT_TWO_PI)) * bell
 
 
 def block_diagonal(square):

time: 109 us -> 109 us (level)
  no operation moved by 1% of the time
where the time goes in v3:
time: 109 us; the launch traced here: 108 us
  blocking collectives  73.8 us (68%)
  Pallas kernels  23.7 us (22%)
  starting transfers between devices  8.53 us (8%)
  waiting for transfers between devices  1.17 us (1%)
    all_to_all x4, blocking collectives, exchange(): return lax.all_to_all(rows, 'gx', 0, 0, tiled=True)  73.8 us
    ppermute x4, starting transfers between devices, swap_cores(): return lax.ppermute(values, 'gy', [(0, 1), (1, 0)])  8.53 us
    pallas_call x1, Pallas kernels, cells_step(): pl.pallas_call(cells_kernel, in_specs=[SMEM] + [VMEM] * 7, out_specs=[VME...  5.8 us
    pallas_call x1, Pallas kernels, last_step(): pl.pallas_call(last_kernel, in_specs=[SMEM] + [VMEM] * 5, out_specs=[pl.B...  4.93 us
    pallas_call x1, Pallas kernels, y_forward(): pl.pallas_call(y_forward_kernel, in_specs=[SMEM, away, away, away], out_s...  4.5 us
  transfers between devices with their start and end apart: 4, of which 1 were waited for; matrix products, arithmetic and copies ran while one was open for 0% of the time, Pallas kernels for 4%

profile of v3, /device:TPU:1, one launch (start us, length us, event | category | flops | bytes accessed | tf_op | source)
XLA Modules:
  0.0 108.2 jit_solution(4543480664897030281)
XLA Ops:
  0.6 0.1 pad_add_fusion.place
  0.7 4.5 %y_forward.1 = (bf16[32,64,1024]{2,1,0:T(8,128)(2,1)S(1)}, bf16[32,32,128]{2,1,0:T(8,128)(2,1)S(1)}, bf16[32,32,128]{2,1,0:T(8,128)(2,1)S(1)}, bf16[1024,128]{1,...) custom-call(s32[2]{0:T(128)S(1)} %pad_add_fusion.place, bf16[64,32,1024]{2,1,0:T(8,128)(2,1)} %bitcast.10, ...), custom_call_target="tpu_custom_call" | custom-call | tf_op jit(solution)/shard_map/y_forward/pallas_call | solution.py:158
  5.2 1.5 %collective-permute-start = (bf16[32,32,128]{2,1,0:T(8,128)(2,1)S(1)}, bf16[32,32,128]{2,1,0:T(8,128)(2,1)S(1)}, u32[]{:S(2)}, u32[]{:S(2)}) collective-permute-start(bf16[32,32,128]{2,1,0:T(8,128)(2,1)S(1)} %get-tuple-element.22), channel_id=1, source_target_pairs={{0,1},{1,0},{2,3},{3,2},{4,5},{5,4},{6,7},{7,6},{8,9},{9,8},{10,11... | collective-permute-start | bytes 786440 | tf_op jit(solution)/shard_map/ppermute | solution.py:567
  6.7 1.2 %collective-permute-done.refs_2_ = bf16[32,32,128]{2,1,0:T(8,128)(2,1)S(1)} collective-permute-done((bf16[32,32,128]{2,1,0:T(8,128)(2,1)S(1)}, bf16[32,32,128]{2,1,0:T(8,128)(2,1)S(1)}, u32[]{:S(2)}, u32[]{:S(2)}) %collective-permute-start) | collective-permute-done | bytes 262176 | tf_op jit(solution)/shard_map/ppermute | solution.py:567
  7.9 0.6 x_forward.2
  8.5 23.3 %all_to_all.20.sent_ref = bf16[64,32,128]{2,1,0:T(8,128)(2,1)S(1)} all-to-all(bf16[64,32,128]{2,1,0:T(8,128)(2,1)S(1)} %x_forward.2), channel_id=1, replica_groups=mesh['gx'=64,'gy'=2] {'gx'}, dimensions={0} | all-to-all | bytes 1048576 | tf_op jit(solution)/shard_map/all_to_all | solution.py:571
  31.7 1.0 mix.1
  32.7 15.4 %all_to_all.21.sent_ref = bf16[64,32,128]{2,1,0:T(8,128)(2,1)S(1)} all-to-all(bf16[64,32,128]{2,1,0:T(8,128)(2,1)S(1)} %get-tuple-element.23), channel_id=1, replica_groups=mesh['gx'=64,'gy'=2] {'gx'}, dimensions={0} | all-to-all | bytes 1048576 | tf_op jit(solution)/shard_map/all_to_all | solution.py:571
  48.1 0.7 x_inverse.2.after_ref.own_in_ref
  48.8 3.4 %collective-permute-start.1 = (bf16[32,32,128]{2,1,0:T(8,128)(2,1)S(1)}, bf16[32,32,128]{2,1,0:T(8,128)(2,1)S(1)}, u32[]{:S(2)}, u32[]{:S(2)}) collective-permute-start(bf16[32,32,128]{2,1,0:T(8,128)(2,1)S(1)} %x_inverse.2.after_ref.own_in_ref), channel_id=1, source_target_pairs={{0,1},{1,0},{2,3},{3,2},{4,5},{5,4},{6,7},{7,6},{8,9},{9,8},{10,11... | collective-permute-start | bytes 786440 | tf_op jit(solution)/shard_map/ppermute | solution.py:567
  52.2 1.2 %relaid.1.cotangent_ref = bf16[32,64,1024]{2,1,0:T(8,128)(2,1)S(1)} custom-call(bf16[64,32,1024]{2,1,0:T(8,128)(2,1)S(1)} %bitcast.7, bf16[32,32,128]{2,1,0:T(8,128)(2,1)S(1)} %x_inverse.2.after_ref.own_in_ref), custom_call_target="tpu_custom_call" | custom-call | flops 1073741824 | bytes 8388608 | tf_op jit(solution)/shard_map/relaid/pallas_call | solution.py:354
  53.5 5.8 %cells_step.1 = (bf16[32,64,1024]{2,1,0:T(8,128)(2,1)S(1)}, bf16[32,32,128]{2,1,0:T(8,128)(2,1)S(1)}, bf16[32,32,128]{2,1,0:T(8,128)(2,1)S(1)}) custom-call(s32[2]{0:T(128)S(1)} %pad_add_fusion.place, bf16[32,64,1024]{2,1,0:T(8,128)(2,1)S(1)} %get-tuple-element.18.field_ref, bf16[32,64,1024]{2,1,0:T(8,128)(2,1)S(1)} %relaid.1.cotangent_ref, ...), custom_call_target="tpu_custom_call" | custom-call | tf_op jit(solution)/shard_map/cells_step/pallas_call | solution.py:483
  59.3 0.5 collective-permute-start.2
  59.8 1.4 %weight_step.1.refs_3_ = bf16[64,128]{1,0:T(8,128)(2,1)S(1)} custom-call(bf16[32,64,1024]{2,1,0:T(8,128)(2,1)S(1)} %get-tuple-element.18.field_ref, bf16[32,64,1024]{2,1,0:T(8,128)(2,1)S(1)} %get-tuple-element.25.slope_ref), custom_call_target="tpu_custom_call" | custom-call | flops 1073741824 | bytes 8388608 | tf_op jit(solution)/shard_map/weight_step/pallas_call | solution.py:379
  61.2 0.0 collective-permute-done.2.refs_2_
  61.3 0.6 x_forward.3
  61.8 18.0 %all_to_all.22.sent_ref = bf16[64,40,128]{2,1,0:T(8,128)(2,1)S(1)} all-to-all(bf16[64,40,128]{2,1,0:T(8,128)(2,1)S(1)} %x_forward.3), channel_id=1, replica_groups=mesh['gx'=64,'gy'=2] {'gx'}, dimensions={0} | all-to-all | bytes 1310720 | tf_op jit(solution)/shard_map/all_to_all | solution.py:571
  79.9 1.0 mix_back.1
  80.9 17.1 %all_to_all.23.sent_ref = bf16[64,40,128]{2,1,0:T(8,128)(2,1)S(1)} all-to-all(bf16[64,40,128]{2,1,0:T(8,128)(2,1)S(1)} %get-tuple-element.28), channel_id=1, replica_groups=mesh['gx'=64,'gy'=2] {'gx'}, dimensions={0} | all-to-all | bytes 1310720 | tf_op jit(solution)/shard_map/all_to_all | solution.py:571
  97.9 0.7 x_inverse.3.own_in_ref
  98.7 3.1 %collective-permute-start.3 = (bf16[34,32,128]{2,1,0:T(8,128)(2,1)S(1)}, bf16[34,32,128]{2,1,0:T(8,128)(2,1)S(1)}, u32[]{:S(2)}, u32[]{:S(2)}) collective-permute-start(bf16[34,32,128]{2,1,0:T(8,128)(2,1)S(1)} %x_inverse.3.own_in_ref), channel_id=1, source_target_pairs={{0,1},{1,0},{2,3},{3,2},{4,5},{5,4},{6,7},{7,6},{8,9},{9,8},{10,11... | collective-permute-start | bytes 835592 | tf_op jit(solution)/shard_map/ppermute | solution.py:567
  101.8 1.3 %outer.1 = f32[32,64,128]{2,1,0:T(8,128)} custom-call(bf16[64,64]{1,0:T(8,128)(2,1)S(1)} %get-tuple-element.30.spectrum_ref, bf16[64,128]{1,0:T(8,128)(2,1)S(1)} %get-tuple-element.31.pair_ref), custom_call_target="tpu_custom_call" | custom-call | flops 1073741824 | bytes 1048576 | tf_op jit(solution)/shard_map/outer/pallas_call | solution.py:337
  103.1 0.0 collective-permute-done.3.other_in_ref
  103.2 4.9 %last_step.1 = (bf16[64,32,1024]{2,1,0:T(8,128)(2,1)}, f32[64,64]{1,0:T(8,128)}) custom-call(s32[2]{0:T(128)S(1)} %pad_add_fusion.place, bf16[32,64,1024]{2,1,0:T(8,128)(2,1)S(1)} %get-tuple-element.25.slope_ref, bf16[34,32,128]{2,1,0:T(8,128)(2,1)S(1)} %x_inverse.3.own_in_ref, bf16[34,32,128]{2,1,0:T(8,128)(2,1)S(1)} %collective-permute-done.3.other_in_ref, ...), custom_call_target="tpu_custom_call" | custom-call | tf_op jit(solution)/shard_map/last_step/pallas_call | solution.py:548
  (9 shorter events, 0.0 us)
Async XLA Ops:
  0.6 31.1 %copy-start.1 = (bf16[1,32,64,128]{3,2,1,0:T(8,128)(2,1)S(1)}, bf16[1,32,64,128]{3,2,1,0:T(8,128)(2,1)}, u32[]{:S(2)}) copy-start(bf16[1,32,64,128]{3,2,1,0:T(8,128)(2,1)} %param.10) | copy-start | bytes 1572868
  0.7 51.5 %copy-start = (bf16[1,64,32,1024]{3,2,1,0:T(8,128)(2,1)S(1)}, bf16[1,64,32,1024]{3,2,1,0:T(8,128)(2,1)}, u32[]{:S(2)}) copy-start(bf16[1,64,32,1024]{3,2,1,0:T(8,128)(2,1)} %param.8) | copy-start | bytes 12582916
  5.2 2.7 %collective-permute-start = (bf16[32,32,128]{2,1,0:T(8,128)(2,1)S(1)}, bf16[32,32,128]{2,1,0:T(8,128)(2,1)S(1)}, u32[]{:S(2)}, u32[]{:S(2)}) collective-permute-start(bf16[32,32,128]{2,1,0:T(8,128)(2,1)S(1)} %get-tuple-element.22), channel_id=1, source_target_pairs={{0,1},{1,0},{2,3},{3,2},{4,5},{5,4},{6,7},{7,6},{8,9},{9,8},{10,11... | collective-permute-start | bytes 786440 | tf_op jit(solution)/shard_map/ppermute | solution.py:567
  48.8 4.6 %collective-permute-start.1 = (bf16[32,32,128]{2,1,0:T(8,128)(2,1)S(1)}, bf16[32,32,128]{2,1,0:T(8,128)(2,1)S(1)}, u32[]{:S(2)}, u32[]{:S(2)}) collective-permute-start(bf16[32,32,128]{2,1,0:T(8,128)(2,1)S(1)} %x_inverse.2.after_ref.own_in_ref), channel_id=1, source_target_pairs={{0,1},{1,0},{2,3},{3,2},{4,5},{5,4},{6,7},{7,6},{8,9},{9,8},{10,11... | collective-permute-start | bytes 786440 | tf_op jit(solution)/shard_map/ppermute | solution.py:567
  52.2 1.3 %copy-start.2 = (bf16[128,1024]{1,0:T(8,128)(2,1)S(1)}, bf16[128,1024]{1,0:T(8,128)(2,1)}, u32[]{:S(2)}) copy-start(bf16[128,1024]{1,0:T(8,128)(2,1)} %constant.15.clone.back_ref) | copy-start | bytes 786436
  52.2 1.3 %copy-start.3 = (bf16[64,64]{1,0:T(8,128)(2,1)S(1)}, bf16[64,64]{1,0:T(8,128)(2,1)}, u32[]{:S(2)}) copy-start(bf16[64,64]{1,0:T(8,128)(2,1)} %local_ref.3) | copy-start | bytes 24580
  59.3 1.9 %collective-permute-start.2 = (bf16[32,32,128]{2,1,0:T(8,128)(2,1)S(1)}, bf16[32,32,128]{2,1,0:T(8,128)(2,1)S(1)}, u32[]{:S(2)}, u32[]{:S(2)}) collective-permute-start(bf16[32,32,128]{2,1,0:T(8,128)(2,1)S(1)} %get-tuple-element.27), channel_id=1, source_target_pairs={{0,1},{1,0},{2,3},{3,2},{4,5},{5,4},{6,7},{7,6},{8,9},{9,8},{10,11... | collective-permute-start | bytes 786440 | tf_op jit(solution)/shard_map/ppermute | solution.py:567
  98.7 4.5 %collective-permute-start.3 = (bf16[34,32,128]{2,1,0:T(8,128)(2,1)S(1)}, bf16[34,32,128]{2,1,0:T(8,128)(2,1)S(1)}, u32[]{:S(2)}, u32[]{:S(2)}) collective-permute-start(bf16[34,32,128]{2,1,0:T(8,128)(2,1)S(1)} %x_inverse.3.own_in_ref), channel_id=1, source_target_pairs={{0,1},{1,0},{2,3},{3,2},{4,5},{5,4},{6,7},{7,6},{8,9},{9,8},{10,11... | collective-permute-start | bytes 835592 | tf_op jit(solution)/shard_map/ppermute | solution.py:567

commit v4 on v3

--- a/solution.py
+++ b/solution.py
@@ -79,7 +79,7 @@
     own = jnp.where(core == 0, half_a, half_b)
     other = jnp.where(core == 0, half_b, half_a)
     shape = (cells, groups * 8, 128)
-    return own.reshape(shape).astype(BF), other.reshape(shape).astype(BF)
+    return own.reshape(shape), other.reshape(shape)
 
 
 def rotated(phase_ref, shard, rows, columns, axis):
@@ -120,13 +120,12 @@
     inverse_ref,
     held,
     phase,
+    kept,
     arrived,
 ):
     def copy(k):
-        group, half = k // 2, k % 2
-        channels = pl.ds(pl.multiple_of(32 * group, 32), 32)
-        cells = pl.ds(pl.multiple_of(16 * half, 16), 16)
-        return pltpu.make_async_copy(field_ref.at[channels, cells], held.at[k], arrived.at[k])
+        channels = pl.ds(pl.multiple_of(16 * k, 16), 16)
+        return pltpu.make_async_copy(field_ref.at[channels], held.at[k], arrived.at[k])
 
     copy_phase = pltpu.make_async_copy(phase_ref, phase, arrived.at[4])
     copy_table = pltpu.make_async_copy(table_ref, forth_ref, arrived.at[5])
@@ -140,16 +139,16 @@
 
     @pl.loop(0, 4)
     def _(k):
-        group, half = k // 2, k % 2
         copy(k).wait()
         rows = jnp.swapaxes(held[k], 0, 1)
-        cells = pl.ds(pl.multiple_of(16 * half, 16), 16)
-        cells_ref[cells, pl.ds(pl.multiple_of(32 * group, 32), 32), :] = rows
-        parts = dot(rows.reshape(16 * 32, YC), forth_ref[...])
-        own, other = split_halves(parts, 16, 2, place[1])
-        channels = pl.ds(pl.multiple_of(16 * group, 16), 16)
-        own_ref[cells, channels, :] = own
-        other_ref[cells, channels, :] = other
+        cells_ref[:, pl.ds(pl.multiple_of(16 * k, 16), 16), :] = rows
+        parts = dot(rows.reshape(XC * 16, YC), forth_ref[...])
+        own, other = split_halves(parts, XC, 1, place[1])
+        kept[0, :, pl.ds(pl.multiple_of(8 * k, 8), 8), :] = own
+        kept[1, :, pl.ds(pl.multiple_of(8 * k, 8), 8), :] = other
+
+    other_ref[...] = kept[1].astype(BF)
+    own_ref[...] = kept[0].astype(BF)
 
 
 def y_forward(place, field, forth, phase):
@@ -168,8 +167,9 @@
             pltpu.VMEM((512, 512), BF),
         ],
         scratch_shapes=[
-            pltpu.VMEM((4, 32, 16, YC), BF),
+            pltpu.VMEM((4, 16, XC, YC), BF),
             pltpu.VMEM((2, 160, 128), F32),
+            pltpu.VMEM((2, XC, 32, 128), F32),
             pltpu.SemaphoreType.DMA((6,)),
         ],
         compiler_params=pltpu.CompilerParams(vmem_limit_bytes=16 << 20),
@@ -250,12 +250,21 @@
     return jnp.concatenate(blocks, axis=1)
 
 
+def summed(sent_ref):
+    total = sent_ref[:8].astype(F32)
+    for k in range(1, 8):
+        total = total + sent_ref[8 * k : 8 * k + 8].astype(F32)
+    total = total[:4] + total[4:]
+    total = total[:2] + total[2:]
+    return total[0] + total[1]
+
+
 def own_mode(shape):
     return iota(shape, 1) // C == iota(shape, 0) % 32
 
 
 def mix_kernel(sent_ref, weight_ref, out_ref, spectrum_ref):
-    spectrum = modes_of(jnp.sum(sent_ref[...].astype(F32), axis=0))
+    spectrum = modes_of(summed(sent_ref))
     spectrum_ref[...] = spectrum
     pair = spectrum.astype(F32)
     pair = jnp.concatenate([pair, pair], axis=1)
@@ -282,7 +291,7 @@
 
 
 def mix_back_kernel(sent_ref, weight_ref, out_ref, pair_ref):
-    total = jnp.sum(sent_ref[...].astype(F32), axis=0)
+    total = summed(sent_ref)
     modes = modes_of(total[:32]).astype(F32)
     real, imag = modes[:32], modes[32:]
     left = jnp.concatenate([real, imag], axis=1)
@@ -476,7 +485,8 @@
     for half in range(2):
         cells = slice(16 * half, 16 * half + 16)
         parts = jnp.concatenate([sums[half, g] for g in range(4)], axis=0)
-        own_ref[cells], other_ref[cells] = split_halves(parts, 16, 4, place[1])
+        own, other = split_halves(parts, 16, 4, place[1])
+        own_ref[cells], other_ref[cells] = own.astype(BF), other.astype(BF)
 
 
 def cells_step(place, cells, cotangent, own, other, local_weight, forth, back):

time: 109 us -> 108 us (level)
  no operation moved by 1% of the time
where the time goes in v4:
time: 108 us
  blocking collectives  73.8 us (68%)
  Pallas kernels  23.6 us (22%)
  starting transfers between devices  8.52 us (8%)
  waiting for transfers between devices  1.17 us (1%)
    all_to_all x4, blocking collectives, exchange(): return lax.all_to_all(rows, 'gx', 0, 0, tiled=True)  73.8 us
    ppermute x4, starting transfers between devices, swap_cores(): return lax.ppermute(values, 'gy', [(0, 1), (1, 0)])  8.52 us
    pallas_call x1, Pallas kernels, cells_step(): pl.pallas_call(cells_kernel, in_specs=[SMEM] + [VMEM] * 7, out_specs=[VME...  5.79 us
    pallas_call x1, Pallas kernels, last_step(): pl.pallas_call(last_kernel, in_specs=[SMEM] + [VMEM] * 5, out_specs=[pl.B...  4.93 us
    pallas_call x1, Pallas kernels, y_forward(): pl.pallas_call(y_forward_kernel, in_specs=[SMEM, away, away, away], out_s...  4.46 us
  transfers between devices with their start and end apart: 4, of which 1 were waited for; matrix products, arithmetic and copies ran while one was open for 0% of the time, Pallas kernels for 4%

profile of v4, /device:TPU:1, one launch (start us, length us, event | category | flops | bytes accessed | tf_op | source)
XLA Modules:
  0.0 108.2 jit_solution(10591046757325592627)
XLA Ops:
  0.6 0.1 pad_add_fusion.place
  0.7 4.5 %y_forward.1 = (bf16[32,64,1024]{2,1,0:T(8,128)(2,1)S(1)}, bf16[32,32,128]{2,1,0:T(8,128)(2,1)S(1)}, bf16[32,32,128]{2,1,0:T(8,128)(2,1)S(1)}, bf16[1024,128]{1,...) custom-call(s32[2]{0:T(128)S(1)} %pad_add_fusion.place, bf16[64,32,1024]{2,1,0:T(8,128)(2,1)} %bitcast.10, ...), custom_call_target="tpu_custom_call" | custom-call | tf_op jit(solution)/shard_map/y_forward/pallas_call | solution.py:157
  5.2 1.5 %collective-permute-start = (bf16[32,32,128]{2,1,0:T(8,128)(2,1)S(1)}, bf16[32,32,128]{2,1,0:T(8,128)(2,1)S(1)}, u32[]{:S(2)}, u32[]{:S(2)}) collective-permute-start(bf16[32,32,128]{2,1,0:T(8,128)(2,1)S(1)} %get-tuple-element.22), channel_id=1, source_target_pairs={{0,1},{1,0},{2,3},{3,2},{4,5},{5,4},{6,7},{7,6},{8,9},{9,8},{10,11... | collective-permute-start | bytes 786440 | tf_op jit(solution)/shard_map/ppermute | solution.py:577
  6.7 1.2 %collective-permute-done.refs_2_ = bf16[32,32,128]{2,1,0:T(8,128)(2,1)S(1)} collective-permute-done((bf16[32,32,128]{2,1,0:T(8,128)(2,1)S(1)}, bf16[32,32,128]{2,1,0:T(8,128)(2,1)S(1)}, u32[]{:S(2)}, u32[]{:S(2)}) %collective-permute-start) | collective-permute-done | bytes 262176 | tf_op jit(solution)/shard_map/ppermute | solution.py:577
  7.8 0.6 x_forward.2
  8.4 23.3 %all_to_all.20.sent_ref = bf16[64,32,128]{2,1,0:T(8,128)(2,1)S(1)} all-to-all(bf16[64,32,128]{2,1,0:T(8,128)(2,1)S(1)} %x_forward.2), channel_id=1, replica_groups=mesh['gx'=64,'gy'=2] {'gx'}, dimensions={0} | all-to-all | bytes 1048576 | tf_op jit(solution)/shard_map/all_to_all | solution.py:581
  31.7 0.9 mix.1
  32.6 15.4 %all_to_all.21.sent_ref = bf16[64,32,128]{2,1,0:T(8,128)(2,1)S(1)} all-to-all(bf16[64,32,128]{2,1,0:T(8,128)(2,1)S(1)} %get-tuple-element.23), channel_id=1, replica_groups=mesh['gx'=64,'gy'=2] {'gx'}, dimensions={0} | all-to-all | bytes 1048576 | tf_op jit(solution)/shard_map/all_to_all | solution.py:581
  48.1 0.7 x_inverse.2.after_ref.own_in_ref
  48.8 3.4 %collective-permute-start.1 = (bf16[32,32,128]{2,1,0:T(8,128)(2,1)S(1)}, bf16[32,32,128]{2,1,0:T(8,128)(2,1)S(1)}, u32[]{:S(2)}, u32[]{:S(2)}) collective-permute-start(bf16[32,32,128]{2,1,0:T(8,128)(2,1)S(1)} %x_inverse.2.after_ref.own_in_ref), channel_id=1, source_target_pairs={{0,1},{1,0},{2,3},{3,2},{4,5},{5,4},{6,7},{7,6},{8,9},{9,8},{10,11... | collective-permute-start | bytes 786440 | tf_op jit(solution)/shard_map/ppermute | solution.py:577
  52.2 1.2 %relaid.1.cotangent_ref = bf16[32,64,1024]{2,1,0:T(8,128)(2,1)S(1)} custom-call(bf16[64,32,1024]{2,1,0:T(8,128)(2,1)S(1)} %bitcast.7, bf16[32,32,128]{2,1,0:T(8,128)(2,1)S(1)} %x_inverse.2.after_ref.own_in_ref), custom_call_target="tpu_custom_call" | custom-call | flops 1073741824 | bytes 8388608 | tf_op jit(solution)/shard_map/relaid/pallas_call | solution.py:363
  53.4 0.0 collective-permute-done.1.other_in_ref
  53.4 5.8 %cells_step.1 = (bf16[32,64,1024]{2,1,0:T(8,128)(2,1)S(1)}, bf16[32,32,128]{2,1,0:T(8,128)(2,1)S(1)}, bf16[32,32,128]{2,1,0:T(8,128)(2,1)S(1)}) custom-call(s32[2]{0:T(128)S(1)} %pad_add_fusion.place, bf16[32,64,1024]{2,1,0:T(8,128)(2,1)S(1)} %get-tuple-element.18.field_ref, bf16[32,64,1024]{2,1,0:T(8,128)(2,1)S(1)} %relaid.1.cotangent_ref, ...), custom_call_target="tpu_custom_call" | custom-call | tf_op jit(solution)/shard_map/cells_step/pallas_call | solution.py:493
  59.2 0.5 collective-permute-start.2
  59.8 1.4 %weight_step.1.refs_3_ = bf16[64,128]{1,0:T(8,128)(2,1)S(1)} custom-call(bf16[32,64,1024]{2,1,0:T(8,128)(2,1)S(1)} %get-tuple-element.18.field_ref, bf16[32,64,1024]{2,1,0:T(8,128)(2,1)S(1)} %get-tuple-element.25.slope_ref), custom_call_target="tpu_custom_call" | custom-call | flops 1073741824 | bytes 8388608 | tf_op jit(solution)/shard_map/weight_step/pallas_call | solution.py:388
  61.2 0.0 collective-permute-done.2.refs_2_
  61.2 0.6 x_forward.3
  61.8 18.0 %all_to_all.22.sent_ref = bf16[64,40,128]{2,1,0:T(8,128)(2,1)S(1)} all-to-all(bf16[64,40,128]{2,1,0:T(8,128)(2,1)S(1)} %x_forward.3), channel_id=1, replica_groups=mesh['gx'=64,'gy'=2] {'gx'}, dimensions={0} | all-to-all | bytes 1310720 | tf_op jit(solution)/shard_map/all_to_all | solution.py:581
  79.8 1.0 mix_back.1
  80.8 17.1 %all_to_all.23.sent_ref = bf16[64,40,128]{2,1,0:T(8,128)(2,1)S(1)} all-to-all(bf16[64,40,128]{2,1,0:T(8,128)(2,1)S(1)} %get-tuple-element.28), channel_id=1, replica_groups=mesh['gx'=64,'gy'=2] {'gx'}, dimensions={0} | all-to-all | bytes 1310720 | tf_op jit(solution)/shard_map/all_to_all | solution.py:581
  97.9 0.7 x_inverse.3.own_in_ref
  98.6 3.1 %collective-permute-start.3 = (bf16[34,32,128]{2,1,0:T(8,128)(2,1)S(1)}, bf16[34,32,128]{2,1,0:T(8,128)(2,1)S(1)}, u32[]{:S(2)}, u32[]{:S(2)}) collective-permute-start(bf16[34,32,128]{2,1,0:T(8,128)(2,1)S(1)} %x_inverse.3.own_in_ref), channel_id=1, source_target_pairs={{0,1},{1,0},{2,3},{3,2},{4,5},{5,4},{6,7},{7,6},{8,9},{9,8},{10,11... | collective-permute-start | bytes 835592 | tf_op jit(solution)/shard_map/ppermute | solution.py:577
  101.7 1.3 %outer.1 = f32[32,64,128]{2,1,0:T(8,128)} custom-call(bf16[64,64]{1,0:T(8,128)(2,1)S(1)} %get-tuple-element.30.spectrum_ref, bf16[64,128]{1,0:T(8,128)(2,1)S(1)} %get-tuple-element.31.pair_ref), custom_call_target="tpu_custom_call" | custom-call | flops 1073741824 | bytes 1048576 | tf_op jit(solution)/shard_map/outer/pallas_call | solution.py:346
  103.1 4.9 %last_step.1 = (bf16[64,32,1024]{2,1,0:T(8,128)(2,1)}, f32[64,64]{1,0:T(8,128)}) custom-call(s32[2]{0:T(128)S(1)} %pad_add_fusion.place, bf16[32,64,1024]{2,1,0:T(8,128)(2,1)S(1)} %get-tuple-element.25.slope_ref, bf16[34,32,128]{2,1,0:T(8,128)(2,1)S(1)} %x_inverse.3.own_in_ref, bf16[34,32,128]{2,1,0:T(8,128)(2,1)S(1)} %collective-permute-done.3.other_in_ref, ...), custom_call_target="tpu_custom_call" | custom-call | tf_op jit(solution)/shard_map/last_step/pallas_call | solution.py:558
  (9 shorter events, 0.0 us)
Async XLA Ops:
  0.6 31.1 %copy-start.1 = (bf16[1,32,64,128]{3,2,1,0:T(8,128)(2,1)S(1)}, bf16[1,32,64,128]{3,2,1,0:T(8,128)(2,1)}, u32[]{:S(2)}) copy-start(bf16[1,32,64,128]{3,2,1,0:T(8,128)(2,1)} %param.10) | copy-start | bytes 1572868
  0.7 51.4 %copy-start = (bf16[1,64,32,1024]{3,2,1,0:T(8,128)(2,1)S(1)}, bf16[1,64,32,1024]{3,2,1,0:T(8,128)(2,1)}, u32[]{:S(2)}) copy-start(bf16[1,64,32,1024]{3,2,1,0:T(8,128)(2,1)} %param.8) | copy-start | bytes 12582916
  5.2 2.7 %collective-permute-start = (bf16[32,32,128]{2,1,0:T(8,128)(2,1)S(1)}, bf16[32,32,128]{2,1,0:T(8,128)(2,1)S(1)}, u32[]{:S(2)}, u32[]{:S(2)}) collective-permute-start(bf16[32,32,128]{2,1,0:T(8,128)(2,1)S(1)} %get-tuple-element.22), channel_id=1, source_target_pairs={{0,1},{1,0},{2,3},{3,2},{4,5},{5,4},{6,7},{7,6},{8,9},{9,8},{10,11... | collective-permute-start | bytes 786440 | tf_op jit(solution)/shard_map/ppermute | solution.py:577
  48.8 4.6 %collective-permute-start.1 = (bf16[32,32,128]{2,1,0:T(8,128)(2,1)S(1)}, bf16[32,32,128]{2,1,0:T(8,128)(2,1)S(1)}, u32[]{:S(2)}, u32[]{:S(2)}) collective-permute-start(bf16[32,32,128]{2,1,0:T(8,128)(2,1)S(1)} %x_inverse.2.after_ref.own_in_ref), channel_id=1, source_target_pairs={{0,1},{1,0},{2,3},{3,2},{4,5},{5,4},{6,7},{7,6},{8,9},{9,8},{10,11... | collective-permute-start | bytes 786440 | tf_op jit(solution)/shard_map/ppermute | solution.py:577
  52.2 1.3 %copy-start.2 = (bf16[128,1024]{1,0:T(8,128)(2,1)S(1)}, bf16[128,1024]{1,0:T(8,128)(2,1)}, u32[]{:S(2)}) copy-start(bf16[128,1024]{1,0:T(8,128)(2,1)} %constant.15.clone.back_ref) | copy-start | bytes 786436
  52.2 1.3 %copy-start.3 = (bf16[64,64]{1,0:T(8,128)(2,1)S(1)}, bf16[64,64]{1,0:T(8,128)(2,1)}, u32[]{:S(2)}) copy-start(bf16[64,64]{1,0:T(8,128)(2,1)} %local_ref.3) | copy-start | bytes 24580
  59.2 1.9 %collective-permute-start.2 = (bf16[32,32,128]{2,1,0:T(8,128)(2,1)S(1)}, bf16[32,32,128]{2,1,0:T(8,128)(2,1)S(1)}, u32[]{:S(2)}, u32[]{:S(2)}) collective-permute-start(bf16[32,32,128]{2,1,0:T(8,128)(2,1)S(1)} %get-tuple-element.27), channel_id=1, source_target_pairs={{0,1},{1,0},{2,3},{3,2},{4,5},{5,4},{6,7},{7,6},{8,9},{9,8},{10,11... | collective-permute-start | bytes 786440 | tf_op jit(solution)/shard_map/ppermute | solution.py:577
  98.6 4.5 %collective-permute-start.3 = (bf16[34,32,128]{2,1,0:T(8,128)(2,1)S(1)}, bf16[34,32,128]{2,1,0:T(8,128)(2,1)S(1)}, u32[]{:S(2)}, u32[]{:S(2)}) collective-permute-start(bf16[34,32,128]{2,1,0:T(8,128)(2,1)S(1)} %x_inverse.3.own_in_ref), channel_id=1, source_target_pairs={{0,1},{1,0},{2,3},{3,2},{4,5},{5,4},{6,7},{7,6},{8,9},{9,8},{10,11... | collective-permute-start | bytes 835592 | tf_op jit(solution)/shard_map/ppermute | solution.py:577
